TPU v7x, 128 devices: a whole 4x4x4 slice. The times are simulated.
128 devices in a mesh: dp: 8 (over y_lo, z), ctx: 16 (over y_hi, x, core).
Axes of the slice: x: 4, y: 4 (y_hi: 2, y_lo: 2; y = y_hi * 2 + y_lo), z: 4, core: 2. Of those that a mesh axis runs over, the one named last changes fastest.
Arguments:
- tokens: bfloat16 [16384, 1024], P(('dp', 'ctx')), may hold values from -6 to 6
- cotangent: bfloat16 [16384, 1024], P(('dp', 'ctx')), may hold values from -6 to 6
- block_order: int32 [16], replicated, may hold values from 0 to 15, each once
- routes: int32 [16384, 8], P(('dp', 'ctx')), may hold values from 0 to 31, all different within a row; in each aligned block of 128 rows (0 to 127, 128 to 255, ...) at most 48 rows name the same one
- norm_one: bfloat16 [1024], P(('dp', 'ctx')), may hold values from 0.099609375 to 1.8984375
- w_query: bfloat16 [1024, 1024], P(('dp', 'ctx')), may hold values from -0.1875 to 0.1875
- w_key: bfloat16 [1024, 512], P(('dp', 'ctx')), may hold values from -0.1875 to 0.1875
- w_value: bfloat16 [1024, 512], P(('dp', 'ctx')), may hold values from -0.1875 to 0.1875
- w_out: bfloat16 [1024, 1024], P(('dp', 'ctx')), may hold values from -3 to 3
- norm_two: bfloat16 [1024], P(('dp', 'ctx')), may hold values from 0.099609375 to 1.8984375
- w_router: bfloat16 [1024, 32], P(('dp', 'ctx')), may hold values from -0.09375 to 0.09375
- expert_in: bfloat16 [32, 1024, 1024], P('ctx', 'dp'), may hold values from -0.1875 to 0.1875
- expert_out: bfloat16 [32, 512, 1024], P('ctx', None, 'dp'), may hold values from -1 to 1
Outputs:
- output: float32 [16384, 1024], P(('dp', 'ctx'))
- input_grad: float32 [16384, 1024], P(('dp', 'ctx'))
- grad_norm_one: float32 [1024], P(('dp', 'ctx'))
- grad_w_query: float32 [1024, 1024], P(('dp', 'ctx'))
- grad_w_key: float32 [1024, 512], P(('dp', 'ctx'))
- grad_w_value: float32 [1024, 512], P(('dp', 'ctx'))
- grad_w_out: float32 [1024, 1024], P(('dp', 'ctx'))
- grad_norm_two: float32 [1024], P(('dp', 'ctx'))
- grad_w_router: float32 [1024, 32], P(('dp', 'ctx'))
- grad_expert_in: float32 [32, 1024, 1024], P('ctx', 'dp')
- grad_expert_out: float32 [32, 512, 1024], P('ctx', None, 'dp')
Inputs may be any that keep to these rules, and one draw needn't show every extreme that they name: `routes`: each row names 8 different experts; the rows of one device name any expert at most 48 times, a bound that some block reaches. A permutation; ctx index c holds, in this order, blocks block_order[c] and 31 - block_order[c] of its sequence's 2 * 16 blocks.
All inputs are finite; a program needn't handle non-finite values.
Results may differ from a plain program's by a relative error of at most 0.024.
Values may be sent and summed in bfloat16 or wider, within the bound.
A program may use at most 128 MiB of HBM per device.

v0:
```python
import math

import jax
import jax.numpy as jnp
from jax import lax
from jax.sharding import Mesh
from jax.sharding import PartitionSpec as P

D = 1024
HEADS = 16
KV_HEADS = 8
HEAD_DIM = 64
EXPERTS = 32
FF = 512
TOP = 8
MOST = 48
DP_CTX = ("dp_0", "dp_1", "ctx")
DP = ("dp_0", "dp_1")


epsilon = 1e-06


def in_one_piece(arrays, axis, dim, along):
    columns = [a.reshape(*a.shape[:along], -1) for a in arrays]
    both = jnp.concatenate(columns, axis=along)
    result, at, finished = (lax.all_gather(both, axis, axis=dim, tiled=True), 0, [])
    for a, column in zip(arrays, columns):
        piece = result[..., at : at + column.shape[along]]
        finished.append(piece.reshape(*piece.shape[:along], *a.shape[along:]))
        at += column.shape[along]
    return tuple(finished)


def rows_first(arrays, axis, dims):
    turned = [jnp.moveaxis(a, dim, 0) for a, dim in zip(arrays, dims)]
    widths = [t[0].size for t in turned]
    both = jnp.concatenate([t.reshape(-1, w) for t, w in zip(turned, widths)], axis=1)
    result = lax.all_gather(both, axis, axis=0, tiled=True)
    pieces = jnp.split(result, [sum(widths[:k]) for k in range(1, len(widths))], axis=1)
    return tuple(
        (
            jnp.moveaxis(b.reshape(-1, *t.shape[1:]), 0, dim)
            for b, t, dim in zip(pieces, turned, dims)
        )
    )


def sent_together(arrays, axis, dim, along):
    widths = [a.shape[along] for a in arrays]
    both = jnp.concatenate(arrays, axis=along)
    result = lax.all_gather(both, axis, axis=dim, tiled=True)
    return tuple(jnp.split(result, [sum(widths[:k]) for k in range(1, len(widths))], axis=along))


def in_one_piece_2(arrays, axis, dim, along):
    widths = [a.shape[along] for a in arrays]
    both = jnp.concatenate(arrays, axis=along)
    result = lax.psum_scatter(both, axis, scatter_dimension=dim, tiled=True)
    return tuple(jnp.split(result, [sum(widths[:k]) for k in range(1, len(widths))], axis=along))


def cut_along(value, dim, size):
    before, after = (value.shape[:dim], value.shape[dim + 1 :])
    return jnp.moveaxis(value.reshape(*before, size, -1, *after), dim, 0)


def sum_packed(arrays, axis, dims):
    size = lax.axis_size(axis)
    pieces = [cut_along(a, dim, size) for a, dim in zip(arrays, dims)]
    lines = jnp.concatenate([b.reshape(size, -1) for b in pieces], axis=1)
    rows = max(16, -(-lines.shape[1] // 1024) * 8)
    lines = jnp.pad(lines, ((0, 0), (0, rows * 128 - lines.shape[1]))).reshape(-1, 128)
    line, at, finished = (lax.psum_scatter(lines, axis, tiled=True).reshape(-1), 0, [])
    for b in pieces:
        part = b[0]
        finished.append(line[at : at + part.size].reshape(part.shape))
        at += part.size
    return tuple(finished)


def sum_in_order(pieces, axes, turns):
    lengths = [lax.axis_size(a) for a in axes]
    pieces = pieces.reshape(*lengths, *pieces.shape[1:])
    pieces = pieces.transpose(*turns, *range(len(axes), pieces.ndim))
    pieces = pieces.reshape(-1, *pieces.shape[len(axes) :])
    for k in turns:
        pieces = lax.psum_scatter(pieces, axes[k], scatter_dimension=0, tiled=True)
    return pieces[0]


def summed_rows(value, axes, turns, dim):
    size = lax.axis_size(axes)
    return sum_in_order(cut_along(value, dim, size), axes, turns)


def rotary(values, places, direction):
    half_dim = values.shape[-1] // 2
    inverse = 10000.0 ** (-jnp.arange(half_dim, dtype=jnp.float32) * 2.0 / values.shape[-1])
    angles = places.astype(jnp.float32)[:, None] * inverse[None, :]
    cosine = jnp.cos(angles)[:, None, :]
    sine_part = direction * jnp.sin(angles)[:, None, :]
    front_half = values[..., :half_dim]
    back_half = values[..., half_dim:]
    return jnp.concatenate(
        [front_half * cosine - back_half * sine_part, back_half * cosine + front_half * sine_part],
        axis=-1,
    )


def layout_positions(block_order, ctx_count, half_rows):
    block_pair = jnp.stack([block_order, 2 * ctx_count - 1 - block_order], axis=1)
    within = jnp.arange(half_rows, dtype=jnp.int32)
    return (block_pair[:, :, None] * half_rows + within[None, None, :]).reshape(-1)


def normalize(inputs, gain_values):
    scale_rows = lax.rsqrt(jnp.mean(inputs * inputs, axis=-1, keepdims=True) + epsilon)
    normed = inputs * scale_rows
    return (scale_rows, normed, (normed * gain_values.astype(jnp.float32)).astype(jnp.bfloat16))


def norm_backward(grad_in, normed, scale_rows, gain_values):
    grad_normed = grad_in * gain_values.astype(jnp.float32)
    inner = jnp.mean(grad_normed * normed, axis=-1, keepdims=True)
    return (scale_rows * (grad_normed - normed * inner), jnp.sum(grad_in * normed, axis=0))


def local(
    tokens,
    cotangent,
    block_order,
    routes,
    norm_one,
    w_query,
    w_key,
    w_value,
    w_out,
    norm_two,
    w_router,
    expert_in,
    expert_out,
):
    ctx_size = lax.axis_size("ctx")
    local_rows = tokens.shape[0]
    half_rows = local_rows // 2
    group_size = HEADS // KV_HEADS
    heads_dim = HEADS * HEAD_DIM
    kv_dim = KV_HEADS * HEAD_DIM
    local_experts = expert_in.shape[0]
    seq_rows = ctx_size * local_rows
    block_rows = math.gcd(seq_rows, 512)
    block_count = seq_rows // block_rows
    root_dim = math.sqrt(HEAD_DIM)
    all_places = layout_positions(block_order, ctx_size, half_rows)
    own_places = lax.dynamic_slice_in_dim(
        all_places, lax.axis_index("ctx") * local_rows, local_rows
    )
    attention_params = in_one_piece(
        (norm_one, w_query, w_key, w_value, w_out, norm_two, w_router), DP_CTX, 0, 1
    )
    expert_params = rows_first((expert_in, expert_out), DP, (1, 2))
    gain_one, query_weight, key_weight, value_weight, out_weight, gain_two, router_weight = (
        attention_params
    )
    in_weight, down_weight = expert_params
    tokens_float = tokens.astype(jnp.float32)
    scale_one, normed_one, hidden_one = normalize(tokens_float, gain_one)
    query_flat = jnp.dot(hidden_one, query_weight, preferred_element_type=jnp.float32)
    key_flat = jnp.dot(hidden_one, key_weight, preferred_element_type=jnp.float32)
    value_rows = jnp.dot(hidden_one, value_weight, preferred_element_type=jnp.float32).astype(
        jnp.bfloat16
    )
    query_rot = rotary(query_flat.reshape(local_rows, HEADS, HEAD_DIM), own_places, 1.0).astype(
        jnp.bfloat16
    )
    query_rot = query_rot.reshape(local_rows, KV_HEADS, group_size, HEAD_DIM)
    key_rot = (
        rotary(key_flat.reshape(local_rows, KV_HEADS, HEAD_DIM), own_places, 1.0)
        .astype(jnp.bfloat16)
        .reshape(local_rows, kv_dim)
    )
    key_all, value_all = sent_together((key_rot, value_rows), "ctx", 0, 1)
    key_blocks = key_all.reshape(block_count, block_rows, KV_HEADS, HEAD_DIM)
    value_blocks = value_all.reshape(block_count, block_rows, KV_HEADS, HEAD_DIM)
    place_blocks = all_places.reshape(block_count, block_rows)

    def block_scores(key_block, place_block):
        scores = (
            jnp.einsum("tgrd,sgd->tgrs", query_rot, key_block, preferred_element_type=jnp.float32)
            / root_dim
        )
        allowed = (place_block[None, :] <= own_places[:, None])[:, None, None, :]
        return (scores, allowed)

    def max_step(running, pieces):
        row_max, row_total = running
        scores, allowed = block_scores(pieces[0], pieces[1])
        new_max = jnp.maximum(row_max, jnp.max(jnp.where(allowed, scores, -1e30), axis=-1))
        weights = jnp.where(allowed, jnp.exp(scores - new_max[..., None]), 0.0)
        return ((new_max, row_total * jnp.exp(row_max - new_max) + jnp.sum(weights, axis=-1)), None)

    stat_shape = (local_rows, KV_HEADS, group_size)
    start_stats = (jnp.full(stat_shape, -1e30, jnp.float32), jnp.zeros(stat_shape, jnp.float32))
    (row_max, row_total), _ = lax.scan(max_step, start_stats, (key_blocks, place_blocks))
    log_total = row_max + jnp.log(row_total)

    def probs_of(key_block, place_block):
        scores, allowed = block_scores(key_block, place_block)
        return jnp.where(allowed, jnp.exp(scores - log_total[..., None]), 0.0)

    def out_step(running, pieces):
        probabilities = probs_of(pieces[0], pieces[2]).astype(jnp.bfloat16)
        return (
            running
            + jnp.einsum(
                "tgrs,sgd->tgrd", probabilities, pieces[1], preferred_element_type=jnp.float32
            ),
            None,
        )

    head_zeros = jnp.zeros((local_rows, KV_HEADS, group_size, HEAD_DIM), jnp.float32)
    attended, _ = lax.scan(out_step, head_zeros, (key_blocks, value_blocks, place_blocks))
    attended = attended.reshape(local_rows, heads_dim).astype(jnp.bfloat16)
    residual = tokens_float + jnp.dot(attended, out_weight, preferred_element_type=jnp.float32)
    scale_two, normed_two, hidden_two = normalize(residual, gain_two)
    logits = jnp.dot(hidden_two, router_weight, preferred_element_type=jnp.float32)
    route_match = routes[:, :, None] == jnp.arange(EXPERTS, dtype=jnp.int32)[None, None, :]
    picked = jnp.sum(jnp.where(route_match, logits[:, None, :], 0.0), axis=-1)
    gate_weights = jax.nn.softmax(picked, axis=-1)
    flat_routes = routes.reshape(-1)
    onehot = (flat_routes[:, None] == jnp.arange(EXPERTS, dtype=jnp.int32)[None, :]).astype(
        jnp.int32
    )
    slot_index = jnp.sum((jnp.cumsum(onehot, axis=0) - onehot) * onehot, axis=1)
    destination = flat_routes * MOST + slot_index
    entries = jnp.arange(flat_routes.shape[0], dtype=jnp.int32)
    slot_source = jnp.zeros((EXPERTS * MOST,), jnp.int32).at[destination].set(entries)
    filled = jnp.zeros((EXPERTS * MOST,), jnp.bool_).at[destination].set(True)
    taken = jnp.take(hidden_two, slot_source // TOP, axis=0)
    send_rows = jnp.where(filled[:, None], taken, jnp.zeros_like(taken)).reshape(
        ctx_size, local_experts, MOST, D
    )
    received = lax.all_to_all(send_rows, "ctx", split_axis=0, concat_axis=0, tiled=True)
    gate_up = jnp.einsum("cemd,edf->cemf", received, in_weight, preferred_element_type=jnp.float32)
    gate_part = gate_up[..., :FF]
    up_part = gate_up[..., FF:]
    expert_hidden = (jax.nn.silu(gate_part) * up_part).astype(jnp.bfloat16)
    expert_result = jnp.einsum(
        "cemf,efd->cemd", expert_hidden, down_weight, preferred_element_type=jnp.float32
    ).astype(jnp.bfloat16)
    returned = lax.all_to_all(
        expert_result, "ctx", split_axis=0, concat_axis=0, tiled=True
    ).reshape(EXPERTS * MOST, D)
    picked_rows = (
        jnp.take(returned, destination, axis=0).reshape(local_rows, TOP, D).astype(jnp.float32)
    )
    output = residual + jnp.sum(gate_weights[:, :, None] * picked_rows, axis=1)
    attention_params = in_one_piece(
        (norm_one, w_query, w_key, w_value, w_out, norm_two, w_router), DP_CTX, 0, 1
    )
    expert_params = rows_first((expert_in, expert_out), DP, (1, 2))
    gain_one, query_weight, key_weight, value_weight, out_weight, gain_two, router_weight = (
        attention_params
    )
    in_weight, down_weight = expert_params
    grad_top = cotangent.astype(jnp.float32)
    d_gates = jnp.sum(grad_top[:, None, :] * picked_rows, axis=-1)
    d_result = (
        (gate_weights[:, :, None] * grad_top[:, None, :])
        .astype(jnp.bfloat16)
        .reshape(local_rows * TOP, D)
    )
    d_picked = gate_weights * (d_gates - jnp.sum(gate_weights * d_gates, axis=-1, keepdims=True))
    d_logits = jnp.sum(jnp.where(route_match, d_picked[:, :, None], 0.0), axis=1).astype(
        jnp.bfloat16
    )
    grad_router = jnp.dot(hidden_two.T, d_logits, preferred_element_type=jnp.float32)
    d_hidden_two = jnp.dot(d_logits, router_weight.T, preferred_element_type=jnp.float32)
    d_taken = jnp.take(d_result, slot_source, axis=0)
    d_send = jnp.where(filled[:, None], d_taken, jnp.zeros_like(d_taken)).reshape(
        ctx_size, local_experts, MOST, D
    )
    d_received = lax.all_to_all(d_send, "ctx", split_axis=0, concat_axis=0, tiled=True)
    d_hidden = jnp.einsum(
        "cemd,efd->cemf", d_received, down_weight, preferred_element_type=jnp.float32
    )
    grad_down = jnp.einsum(
        "cemf,cemd->efd", expert_hidden, d_received, preferred_element_type=jnp.float32
    )
    sigmoid_gate = jax.nn.sigmoid(gate_part)
    d_gate = d_hidden * up_part * (sigmoid_gate * (1.0 + gate_part * (1.0 - sigmoid_gate)))
    d_up = d_hidden * jax.nn.silu(gate_part)
    d_gate_up = jnp.concatenate([d_gate, d_up], axis=-1).astype(jnp.bfloat16)
    grad_in = jnp.einsum("cemd,cemf->edf", received, d_gate_up, preferred_element_type=jnp.float32)
    d_rows = jnp.einsum(
        "cemf,edf->cemd", d_gate_up, in_weight, preferred_element_type=jnp.float32
    ).astype(jnp.bfloat16)
    d_returned = lax.all_to_all(d_rows, "ctx", split_axis=0, concat_axis=0, tiled=True).reshape(
        EXPERTS * MOST, D
    )
    d_hidden_two = d_hidden_two + jnp.sum(
        jnp.take(d_returned, destination, axis=0).reshape(local_rows, TOP, D).astype(jnp.float32),
        axis=1,
    )
    d_norm_two, grad_gain_two = norm_backward(d_hidden_two, normed_two, scale_two, gain_two)
    d_residual = grad_top + d_norm_two
    d_branch = d_residual.astype(jnp.bfloat16)
    grad_out_weight = jnp.dot(attended.T, d_branch, preferred_element_type=jnp.float32)
    d_attended = jnp.dot(d_branch, out_weight.T, preferred_element_type=jnp.float32).astype(
        jnp.bfloat16
    )
    d_attended = d_attended.reshape(local_rows, KV_HEADS, group_size, HEAD_DIM)

    def delta_step(running, pieces):
        probabilities = probs_of(pieces[0], pieces[2])
        d_probs = jnp.einsum(
            "tgrd,sgd->tgrs", d_attended, pieces[1], preferred_element_type=jnp.float32
        )
        return (running + jnp.sum(probabilities * d_probs, axis=-1), None)

    delta, _ = lax.scan(
        delta_step, jnp.zeros(stat_shape, jnp.float32), (key_blocks, value_blocks, place_blocks)
    )

    def grad_step(running, pieces):
        key_block, value_block, place_block = pieces
        probabilities = probs_of(key_block, place_block)
        d_probs = jnp.einsum(
            "tgrd,sgd->tgrs", d_attended, value_block, preferred_element_type=jnp.float32
        )
        d_scores = (probabilities * (d_probs - delta[..., None])).astype(jnp.bfloat16)
        d_query_part = jnp.einsum(
            "tgrs,sgd->tgrd", d_scores, key_block, preferred_element_type=jnp.float32
        )
        d_key_block = jnp.einsum(
            "tgrs,tgrd->sgd", d_scores, query_rot, preferred_element_type=jnp.float32
        )
        d_value_block = jnp.einsum(
            "tgrs,tgrd->sgd",
            probabilities.astype(jnp.bfloat16),
            d_attended,
            preferred_element_type=jnp.float32,
        )
        return (running + d_query_part, (d_key_block, d_value_block))

    d_query_rot, (d_key_blocks, d_value_blocks) = lax.scan(
        grad_step, head_zeros, (key_blocks, value_blocks, place_blocks)
    )
    d_key_all = d_key_blocks.reshape(seq_rows, kv_dim) / root_dim
    d_value_all = d_value_blocks.reshape(seq_rows, kv_dim)
    d_key_own, d_value_own = tuple(
        (
            part.astype(jnp.float32)
            for part in in_one_piece_2(
                (d_key_all.astype(jnp.bfloat16), d_value_all.astype(jnp.bfloat16)), "ctx", 0, 1
            )
        )
    )
    d_query_flat = (
        rotary((d_query_rot / root_dim).reshape(local_rows, HEADS, HEAD_DIM), own_places, -1.0)
        .astype(jnp.bfloat16)
        .reshape(local_rows, heads_dim)
    )
    d_key_flat = (
        rotary(d_key_own.reshape(local_rows, KV_HEADS, HEAD_DIM), own_places, -1.0)
        .astype(jnp.bfloat16)
        .reshape(local_rows, kv_dim)
    )
    d_value_flat = d_value_own.astype(jnp.bfloat16)
    grad_query = jnp.dot(hidden_one.T, d_query_flat, preferred_element_type=jnp.float32)
    grad_key = jnp.dot(hidden_one.T, d_key_flat, preferred_element_type=jnp.float32)
    grad_value = jnp.dot(hidden_one.T, d_value_flat, preferred_element_type=jnp.float32)
    d_hidden_one = jnp.dot(d_query_flat, query_weight.T, preferred_element_type=jnp.float32)
    d_hidden_one = d_hidden_one + jnp.dot(
        d_key_flat, key_weight.T, preferred_element_type=jnp.float32
    )
    d_hidden_one = d_hidden_one + jnp.dot(
        d_value_flat, value_weight.T, preferred_element_type=jnp.float32
    )
    d_norm_one, grad_gain_one = norm_backward(d_hidden_one, normed_one, scale_one, gain_one)
    input_grad = d_residual + d_norm_one
    shard_grads = sum_packed(
        (
            grad_gain_one,
            grad_query,
            grad_key,
            grad_value,
            grad_out_weight,
            grad_gain_two,
            grad_router,
        ),
        DP_CTX,
        (0, 0, 0, 0, 0, 0, 0),
    )
    expert_grads = (
        summed_rows(grad_in.astype(jnp.bfloat16), DP, (1, 0), 1).astype(jnp.float32),
        summed_rows(grad_down.astype(jnp.bfloat16), DP, (1, 0), 2).astype(jnp.float32),
    )
    return (
        output,
        input_grad,
        shard_grads[0],
        shard_grads[1],
        shard_grads[2],
        shard_grads[3],
        shard_grads[4],
        shard_grads[5],
        shard_grads[6],
        expert_grads[0],
        expert_grads[1],
    )


def solution(mesh):
    split = Mesh(mesh.devices.reshape(2, 4, mesh.shape["ctx"]), ("dp_0", "dp_1", "ctx"))
    return jax.shard_map(
        local,
        mesh=split,
        in_specs=(
            P(DP_CTX, None),
            P(DP_CTX, None),
            P(),
            P(DP_CTX, None),
            P(DP_CTX),
            P(DP_CTX, None),
            P(DP_CTX, None),
            P(DP_CTX, None),
            P(DP_CTX, None),
            P(DP_CTX),
            P(DP_CTX, None),
            P("ctx", DP, None),
            P("ctx", None, DP),
        ),
        out_specs=(
            P(DP_CTX, None),
            P(DP_CTX, None),
            P(DP_CTX),
            P(DP_CTX, None),
            P(DP_CTX, None),
            P(DP_CTX, None),
            P(DP_CTX, None),
            P(DP_CTX),
            P(DP_CTX, None),
            P("ctx", DP, None),
            P("ctx", None, DP),
        ),
        check_vma=False,
    )
```

profile of v0, /device:TPU:1, one launch (start us, length us, event | category | flops | bytes accessed | tf_op | source)
XLA Modules:
  0.0 1482.5 jit_solution(6020464922027654373)
XLA Ops:
  13.9 201.0 %all-gather.4.cloned.1.call-done = bf16[1024,3106]{1,0:T(8,128)(2,1)} async-done(((bf16[8,3106]{1,0:T(8,128)(2,1)}), bf16[1024,3106]{1,0:T(8,128)(2,1)}) %all-gather.4.cloned.1.call-update) | async-done | bytes 6361104 | tf_op jit(solution)/shard_map/all_gather | solution.py:27
  223.4 9.0 reduce-window.6
  233.1 4.3 scatter_custom_fusion.1
  237.6 4.6 scatter_custom_fusion
  242.3 3.7 fusion.100
  246.1 31.0 %all-gather.6.cloned.1.call-done = bf16[2048,1024]{1,0:T(8,128)(2,1)} async-done(((bf16[128,1024]{1,0:T(8,128)(2,1)}), bf16[2048,1024]{1,0:T(8,128)(2,1)}) %all-gather.6.cloned.1.call-update) | async-done | bytes 4194320 | tf_op jit(solution)/shard_map/all_gather | solution.py:52
  277.0 3.8 fusion.158
  280.9 3.6 reshape.691
  284.5 4.5 copy.142
  289.0 6.2 reshape.690
  295.2 5.5 copy.141
  300.7 24.2 %while.50 = (s32[]{:T(128)}, f32[128,8,2]{0,2,1:T(2,128)S(1)}, f32[128,8,2]{0,2,1:T(2,128)S(1)}, s32[4,512]{1,0:T(4,128)S(1)}, s32[128]{0:T(128)S(1)}, /*index=5...) while((s32[]{:T(128)}, f32[128,8,2]{0,2,1:T(2,128)S(1)}, ...), condition=%wide.region_4.5_spmd.clone, body=%wide.region_1.4_spmd.clone.sunk | while | flops 141633536 | bytes 9484912 | solution.py:205
  324.9 10.3 while.51
  335.3 3.6 multiply_reduce_fusion.2
  339.9 5.9 gather_fusion
  345.7 3.4 select_select_fusion.1
  349.2 4.5 all-to-all-start
  353.7 4.6 split.29
  358.2 6.3 copy.149
  367.6 27.9 %all-to-all-done = bf16[16,2,48,1024]{3,2,1,0:T(8,128)(2,1)S(1)} async-done(((bf16[16,2,48,1024]{3,2,1,0:T(8,128)(2,1)}), bf16[16,2,48,1024]{3,2,1,0:T(8,128)(2,1)S(1)}, u32[]{:S(2)}, u32[]{:S(2)}) %all-to-all-start) | async-done | bytes 3145760 | tf_op jit(solution)/shard_map/all_to_all | solution.py:244
  395.4 6.4 fusion.85
  408.9 6.3 all-to-all-start.1
  418.6 38.5 %all-to-all-done.1 = bf16[16,2,48,1024]{3,2,1,0:T(8,128)(2,1)S(1)} async-done(((bf16[16,2,48,1024]{3,2,1,0:T(8,128)(2,1)}), bf16[16,2,48,1024]{3,2,1,0:T(8,128)(2,1)S(1)}, u32[]{:S(2)}, u32[]{:S(2)}) %all-to-all-start.1) | async-done | bytes 3145760 | tf_op jit(solution)/shard_map/all_to_all | solution.py:252
  457.1 5.3 gather_fusion.2
  465.7 5.8 gather_fusion.1
  473.7 45.9 %all_to_all.20 = bf16[16,2,48,1024]{3,2,1,0:T(8,128)(2,1)S(1)} all-to-all(bf16[16,2,48,1024]{3,2,1,0:T(8,128)(2,1)S(1)} %select_select_fusion), channel_id=1, replica_groups=mesh['dp_0'=2,'dp_1'=4,'ctx'=16] {'ctx'}, dimensions={0} | all-to-all | bytes 6291456 | tf_op jit(solution)/shard_map/all_to_all | solution.py:284
  524.1 5.8 fusion.76
  529.9 3.7 convert_bitcast_fusion.1
  535.6 4.5 all-to-all-start.3
  540.3 6.4 bitcast_convert_fusion
  549.5 32.4 %all-to-all-done.3 = bf16[16,2,48,1024]{3,2,1,0:T(8,128)(2,1)S(1)} async-done(((bf16[16,2,48,1024]{3,2,1,0:T(8,128)(2,1)}), bf16[16,2,48,1024]{3,2,1,0:T(8,128)(2,1)S(1)}, u32[]{:S(2)}, u32[]{:S(2)}) %all-to-all-start.3) | async-done | bytes 3145760 | tf_op jit(solution)/shard_map/all_to_all | solution.py:299
  581.9 5.3 gather_fusion.3
  587.2 4.6 convert_reduce_fusion
  598.0 17.6 %while.52 = (s32[]{:T(128)}, f32[128,8,2]{0,2,1:T(2,128)S(1)}, s32[4,512]{1,0:T(4,128)S(1)}, s32[128]{0:T(128)S(1)}, bf16[4,512,8,64]{1,3,2,0:T(8,128)(2,1)}, /*...) while((s32[]{:T(128)}, f32[128,8,2]{0,2,1:T(2,128)S(1)}, ...), condition=%wide.region_24.26_spmd.clone, body=%wide.region_22.25_spmd.clone.sunk | while | flops 273745920 | bytes 10141307 | solution.py:322
  615.6 48.8 %while.53 = (s32[]{:T(128)}, f32[128,8,2,64]{0,3,2,1:T(8,128)S(1)}, f32[4,512,8,64]{1,3,2,0:T(8,128)}, bf16[4,512,8,64]{1,3,2,0:T(8,128)(2,1)}, bf16[4,512,8,64]...) while((s32[]{:T(128)}, f32[128,8,2,64]{0,3,2,1:T(8,128)S(1)}, ...), condition=%wide.region_26.28_spmd.clone, body=%wide.region_25.27_spmd.clone.sunk | while | flops 681902080 | bytes 41649328 | solution.py:347
  623.8 3.9 fusion.247
  635.9 3.9 fusion.247
  648.1 3.9 fusion.247
  660.2 3.9 fusion.247
  669.4 3.2 copy.164
  676.0 6.4 copy.189
  686.4 5.0 reshape_reshape.19
  695.2 5.4 reshape_reshape.16
  703.6 58.9 %reduce-scatter.20.cloned.1.call-done = bf16[128,1024]{1,0:T(8,128)(2,1)} async-done(((bf16[2048,1024]{1,0:T(8,128)(2,1)}), bf16[128,1024]{1,0:T(8,128)(2,1)}) %reduce-scatter.20.cloned.1.call-update) | async-done | bytes 262160
  775.9 15.3 %concatenate.57 = f32[128,24848]{1,0:T(8,128)} concatenate(f32[128,8]{1,0:T(8,128)S(1)} %reshape.596, f32[128,8192]{1,0:T(8,128)} %reshape_reshape.16, f32[128,4096]{1,0:T(8,128)S(1)} %reshape_reshape.17, f32[128,4096]{1,0:T(8,128)} %reshape_reshape.18, f32[128,8192]{1,0:T(8,128)} %reshape_reshape.19, f32[128,8]{1,0:T(8,128)S(1)} %reshape.597, f32[128,256]{1,0:T(8,128)S(1)} %reshape_reshape.20), dimensions={1} | concatenate | bytes 25444352 | tf_op jit(solution)/shard_map/concatenate | solution.py:71
  791.3 11.1 pad.4
  802.3 12.2 reshape.598
  819.6 649.0 %reduce-scatter.22.cloned.1.call-done = f32[200,128]{1,0:T(8,128)} async-done(((f32[25600,128]{1,0:T(8,128)}), f32[200,128]{1,0:T(8,128)}) %reduce-scatter.22.cloned.1.call-update) | async-done | bytes 102416
  (313 shorter events, 179.8 us)
Async XLA Ops:
  7.2 211.9 %copy-start.5 = (bf16[128,1024]{1,0:T(8,128)(2,1)S(1)}, bf16[128,1024]{1,0:T(8,128)(2,1)}, u32[]{:S(2)}) copy-start(bf16[128,1024]{1,0:T(8,128)(2,1)} %param.23) | copy-start | bytes 786436
  7.2 207.7 %all-gather.4.cloned.1.call-start = ((), (), s32[]{:S(2)}) async-start(), calls=%async_computation.10 | async-start | bytes 6604800 | tf_op jit(solution)/shard_map/all_gather | solution.py:27
  10.3 266.8 %all-gather.6.cloned.1.call-start = ((), (), s32[]{:S(2)}) async-start(), calls=%async_computation.11 | async-start | bytes 4456448 | tf_op jit(solution)/shard_map/all_gather | solution.py:52
  12.0 209.8 %copy-start.22 = (bf16[2,128,1024]{2,1,0:T(8,128)(2,1)S(1)}, bf16[2,128,1024]{2,1,0:T(8,128)(2,1)}, u32[]{:S(2)}) copy-start(bf16[2,128,1024]{2,1,0:T(8,128)(2,1)} %param.34) | copy-start | bytes 1572868
  13.1 229.1 %copy-start.31 = (f32[128]{0:T(128)}, f32[128]{0:T(128)S(1)}, u32[]{:S(2)}) copy-start(f32[128]{0:T(128)S(1)} %add_rsqrt_fusion.1) | copy-start | bytes 1540
  13.9 232.1 %copy-start.23 = (f32[128,32]{0,1:T(8,128)}, f32[128,32]{0,1:T(8,128)S(1)}, u32[]{:S(2)}) copy-start(f32[128,32]{0,1:T(8,128)S(1)} %get-tuple-element.585) | copy-start | bytes 49156
  216.3 26.0 %copy-start.28 = (f32[1024]{0:T(1024)}, f32[1024]{0:T(1024)S(1)}, u32[]{:S(2)}) copy-start(f32[1024]{0:T(1024)S(1)} %get-tuple-element.475) | copy-start | bytes 12292
  216.3 5.7 copy-start.26
  218.9 4.2 copy-start.30
  221.7 132.0 %all-gather.8.cloned.1.call-start = ((), (), s32[]{:S(2)}) async-start(), calls=%async_computation.12 | async-start | bytes 7077888 | tf_op jit(solution)/shard_map/all_gather | solution.py:39
  335.3 3.7 copy-start
  335.3 10.5 copy-start.3
  335.3 3.6 copy-start.16
  349.2 46.3 %all-to-all-start = ((bf16[16,2,48,1024]{3,2,1,0:T(8,128)(2,1)}), bf16[16,2,48,1024]{3,2,1,0:T(8,128)(2,1)S(1)}, u32[]{:S(2)}, u32[]{:S(2)}) async-start(bf16[16,2,48,1024]{3,2,1,0:T(8,128)(2,1)} %select_select_fusion.1), calls=%async_computation | async-start | bytes 6291456 | tf_op jit(solution)/shard_map/all_to_all | solution.py:244
  395.4 6.4 copy-start.15
  401.9 2.9 copy-start.9
  401.9 3.2 copy-start.18
  404.7 2.1 copy-start.19
  408.9 48.2 %all-to-all-start.1 = ((bf16[16,2,48,1024]{3,2,1,0:T(8,128)(2,1)}), bf16[16,2,48,1024]{3,2,1,0:T(8,128)(2,1)S(1)}, u32[]{:S(2)}, u32[]{:S(2)}) async-start(bf16[16,2,48,1024]{3,2,1,0:T(8,128)(2,1)} %copy.152), calls=%async_computation.1 | async-start | bytes 6291456 | tf_op jit(solution)/shard_map/all_to_all | solution.py:252
  415.2 267.3 %reduce-scatter.16.cloned.1.call-start = ((), (), s32[]{:S(2)}) async-start(), calls=%async_computation.15 | async-start | bytes 2621440 | tf_op jit(solution)/shard_map/reduce_scatter | solution.py:88
  462.4 3.0 copy-start.10
  473.7 46.0 %copy-start.20 = (bf16[16,2,48,512]{3,2,0,1:T(8,128)(2,1)S(1)}, bf16[16,2,48,512]{3,2,0,1:T(8,128)(2,1)}, u32[]{:S(2)}) copy-start(bf16[16,2,48,512]{3,2,0,1:T(8,128)(2,1)} %copy-done.19) | copy-start | bytes 4718596
  524.1 5.8 copy-start.14
  529.9 3.7 copy-start.33
  529.9 3.7 copy-start.34
  535.6 46.3 %all-to-all-start.3 = ((bf16[16,2,48,1024]{3,2,1,0:T(8,128)(2,1)}), bf16[16,2,48,1024]{3,2,1,0:T(8,128)(2,1)S(1)}, u32[]{:S(2)}, u32[]{:S(2)}) async-start(bf16[16,2,48,1024]{3,2,1,0:T(8,128)(2,1)} %copy.157), calls=%async_computation.3 | async-start | bytes 6291456 | tf_op jit(solution)/shard_map/all_to_all | solution.py:299
  540.1 151.4 %reduce-scatter.12.cloned.1.call-start = ((), (), s32[]{:S(2)}) async-start(), calls=%async_computation.13 | async-start | bytes 5242880 | tf_op jit(solution)/shard_map/reduce_scatter | solution.py:88
  549.2 213.3 %reduce-scatter.20.cloned.1.call-start = ((), (), s32[]{:S(2)}) async-start(), calls=%async_computation.17 | async-start | bytes 4456448
  587.2 4.6 copy-start.8
  587.2 6.0 copy-start.21
  593.2 4.8 copy-start.1
  598.0 17.6 %copy-start.4 = (f32[128,8,2,64]{0,3,2,1:T(8,128)S(1)}, f32[128,8,2,64]{0,3,2,1:T(8,128)}, u32[]{:S(2)}) copy-start(f32[128,8,2,64]{0,3,2,1:T(8,128)} %custom-call.4) | copy-start | bytes 1572868
  617.4 3.1 copy-start.2
  629.5 3.1 copy-start.2
  641.6 3.1 copy-start.2
  653.8 3.1 copy-start.2
  682.4 1.3 copy-start.12
  682.4 1.3 copy-start.17
  682.4 132.2 %reduce-scatter.18.cloned.1.call-start = ((), (), s32[]{:S(2)}) async-start(), calls=%async_computation.16 | async-start | bytes 786432 | tf_op jit(solution)/shard_map/reduce_scatter | solution.py:88
  683.2 134.3 %reduce-scatter.14.cloned.1.call-start = ((), (), s32[]{:S(2)}) async-start(), calls=%async_computation.14 | async-start | bytes 1572864 | tf_op jit(solution)/shard_map/reduce_scatter | solution.py:88
  686.3 5.0 copy-start.24
  686.3 5.1 copy-start.27
  691.3 1.0 copy-start.6
  691.3 1.0 copy-start.29
  691.3 1.0 copy-start.32
  691.6 777.0 %reduce-scatter.22.cloned.1.call-start = ((), (), s32[]{:S(2)}) async-start(), calls=%async_computation.18 | async-start | bytes 13209600
  763.6 3.6 copy-start.25
  814.5 1.9 copy-start.13
  (2 other events, 1.6 us)
Sparse Core Ops, SparseCore 0:
  10.4 204.4 all-gather.3
  221.8 55.1 all-gather.5
  279.2 74.1 all-gather.7
  524.2 27.6 reduce-scatter.15
  554.2 46.5 reduce-scatter.11
  682.5 79.9 reduce-scatter.19
  765.0 17.3 reduce-scatter.17
  784.7 23.7 reduce-scatter.13
  814.7 653.8 reduce-scatter.21
where the time goes:
time: 1500 us; the launch traced here: 1480 us
  waiting for transfers between devices  1040 us (69%)
  local copies, waits for them, and re-layouts  162 us (11%)
  matrix products  144 us (10%)
  other arithmetic  58.6 us (4%)
  blocking collectives  45.9 us (3%)
  starting transfers between devices  15.9 us (1%)
  between operations  15.4 us (1%)
    unnamed x11, waiting for transfers between devices  709 us
    all_gather x1, waiting for transfers between devices, in_one_piece(): lax.all_gather(both, axis, axis=dim, tiled=True)  201 us
    all_to_all x1, blocking collectives, local(): lax.all_to_all(d_send, 'ctx', split_axis=0, concat_axis=0, tiled=True)  45.9 us
    all_to_all x1, waiting for transfers between devices, local(): lax.all_to_all(expert_result, 'ctx', split_axis=0, concat_axis=0, tiled=T...  38.5 us
    all_to_all x1, waiting for transfers between devices, local(): lax.all_to_all(d_rows, 'ctx', split_axis=0, concat_axis=0, tiled=True)  32.4 us
    all_gather x1, waiting for transfers between devices, sent_together(): result = lax.all_gather(both, axis, axis=dim, tiled=True)  31 us
  transfers between devices with their start and end apart: 12, of which 7 were waited for; matrix products, arithmetic and copies ran while one was open for 21% of the time, Pallas kernels for 0%

commit v1 on v0

v1 whole, which is shorter than its diff:
```python
import functools
import math

import jax
import jax.numpy as jnp
import numpy as np
from jax import lax
from jax.experimental import pallas as pl
from jax.experimental.pallas import tpu as pltpu
from jax.sharding import Mesh
from jax.sharding import PartitionSpec as P

D = 1024
HEADS = 16
KV_HEADS = 8
HEAD_DIM = 64
EXPERTS = 32
FF = 512
TOP = 8
MOST = 48
ROWS = 128
SEQ = 2048
BLOCK = 64
AXES = ("ylo", "z", "yhi", "x", "core")
DP = ("ylo", "z")
CTX = ("yhi", "x", "core")
N_DP = 8
N_CTX = 16
EXTRA = 128
MESH_ID = pl.DeviceIdType.MESH
ANY = pl.BlockSpec(memory_space=pl.ANY)
VMEM = pl.BlockSpec(memory_space=pltpu.VMEM)
SMEM = pl.BlockSpec(memory_space=pltpu.SMEM)
DMA = pltpu.SemaphoreType.DMA
bf16 = jnp.bfloat16
f32 = jnp.float32
epsilon = 1e-06
CHIPS = [(0, 1), (1, 0), (0, 3), (1, 1), (1, 3), (0, 2), (1, 2)]


def dot(a, b):
    return jnp.dot(a, b, preferred_element_type=f32)


def dot_last(a, b):
    return lax.dot_general(a, b, (((1,), (1,)), ((), ())), preferred_element_type=f32)


def dot_first(a, b):
    return lax.dot_general(a, b, (((0,), (0,)), ((), ())), preferred_element_type=f32)


def my_place():
    return tuple(lax.axis_index(a) for a in AXES)


def device_at(dp, ctx):
    return (
        lax.div(dp, 4),
        lax.rem(dp, 4),
        lax.div(ctx, 8),
        lax.rem(lax.div(ctx, 2), 4),
        lax.rem(ctx, 2),
    )


def chip_peer(place, n):
    ylo, z, yhi, x, core = place
    dy, dx = CHIPS[n]
    return (ylo, z, lax.rem(yhi + dy, 2), lax.rem(x + dx, 4), core)


def chip_from(place, n):
    ylo, z, yhi, x, core = place
    dy, dx = CHIPS[n]
    return (ylo, z, lax.rem(yhi + dy, 2), lax.rem(x + 4 - dx, 4), core)


def ctx_of(place):
    return place[2] * 8 + place[3] * 2 + place[4]


def dp_of(place):
    return place[0] * 4 + place[1]


def sibling_of(place):
    return place[:4] + (1 - place[4],)


def remote(src, dst, send, recv, device):
    return pltpu.make_async_remote_copy(
        src_ref=src, dst_ref=dst, send_sem=send, recv_sem=recv, device_id=device, device_id_type=MESH_ID
    )


def greet(devices):
    barrier = pltpu.get_barrier_semaphore()
    for device in devices:
        pl.semaphore_signal(barrier, inc=1, device_id=device, device_id_type=MESH_ID)
    return barrier


class RowGather:
    scratch = [DMA, DMA((8,)), DMA((8,)), DMA((7,)), DMA((7,))]

    def __init__(self, place, x_ref, out_ref, local, send, recv, fsend, frecv):
        me = ctx_of(place)
        sibling = sibling_of(place)
        self.own = pltpu.make_async_copy(x_ref, out_ref.at[me], local)
        self.out = [
            remote(x_ref, out_ref.at[me], send.at[n], recv.at[n], chip_peer(place, n)) for n in range(7)
        ]
        self.out.append(remote(x_ref, out_ref.at[me], send.at[7], recv.at[7], sibling))
        self.forward = []
        for n in range(7):
            piece = out_ref.at[ctx_of(chip_from(place, n))]
            self.forward.append(remote(piece, piece, fsend.at[n], frecv.at[n], sibling))

    def start(self):
        for copy in self.out:
            copy.start()
        self.own.start()

    def pass_on(self):
        for n in range(7):
            self.out[n].wait_recv()
            self.forward[n].start()

    def finish(self):
        self.own.wait()
        self.out[7].wait_recv()
        for n in range(7):
            self.forward[n].wait_recv()
        for copy in self.out + self.forward:
            copy.wait_send()


def greet_chips(place):
    barrier = greet([chip_peer(place, n) for n in range(7)] + [sibling_of(place)])
    pl.semaphore_wait(barrier, 8)


def gather_kernel(x_ref, out_ref, *sems):
    place = my_place()
    greet_chips(place)
    gather = RowGather(place, x_ref, out_ref, *sems)
    gather.start()
    gather.pass_on()
    gather.finish()


def gather_ctx(x, number):
    return pl.pallas_call(
        gather_kernel,
        out_shape=jax.ShapeDtypeStruct((N_CTX,) + x.shape, x.dtype),
        in_specs=[ANY],
        out_specs=ANY,
        scratch_shapes=RowGather.scratch,
        compiler_params=pltpu.CompilerParams(collective_id=number, has_side_effects=True),
        name="gather_rows",
    )(x)


def scatter_kernel(p_ref, out_ref, own, other, landed, own_sem, send, recv, csend, crecv):
    place = my_place()
    core = place[4]
    sibling = sibling_of(place)
    greet_chips(place)
    mine, cross = [], []
    for n in range(8):
        chip = lax.div(ctx_of(chip_peer(place, n) if n < 7 else place), 2)
        mine.append(pltpu.make_async_copy(p_ref.at[chip, core], own.at[n], own_sem.at[n]))
        cross.append(remote(p_ref.at[chip, 1 - core], other.at[n], send.at[n], recv.at[n], sibling))
    for n in range(8):
        cross[n].start()
        mine[n].start()
    out = []
    for n in range(7):
        mine[n].wait()
        cross[n].wait_recv()
        own[n] = (own[n].astype(f32) + other[n].astype(f32)).astype(bf16)
        copy = remote(own.at[n], landed.at[n], csend.at[n], crecv.at[n], chip_peer(place, n))
        copy.start()
        out.append(copy)
    mine[7].wait()
    cross[7].wait_recv()
    out_ref[...] = own[7].astype(f32) + other[7].astype(f32)
    for n in range(7):
        out[n].wait_recv()
        out_ref[...] += landed[n].astype(f32)
    for n in range(7):
        out[n].wait_send()
    for n in range(8):
        cross[n].wait_send()


def scatter_ctx(parts, number):
    rows, width = parts.shape[-2:]
    parts = parts.reshape(8, 2, rows, width)
    return pl.pallas_call(
        scatter_kernel,
        out_shape=jax.ShapeDtypeStruct((rows, width), f32),
        in_specs=[ANY],
        out_specs=VMEM,
        scratch_shapes=[
            pltpu.VMEM((8, rows, width), bf16),
            pltpu.VMEM((8, rows, width), bf16),
            pltpu.VMEM((7, rows, width), bf16),
            DMA((8,)),
            DMA((8,)),
            DMA((8,)),
            DMA((7,)),
            DMA((7,)),
        ],
        compiler_params=pltpu.CompilerParams(
            collective_id=number, has_side_effects=True, vmem_limit_bytes=24 * 2**20
        ),
        name="scatter_rows",
    )(parts)


def entry_kernel(x_ref, w_ref, o_ref, x_out, w_out, o_out, *sems):
    row_sems, rest = sems[:5], sems[5:]
    wlocal, wsend, wrecv, psend, precv, olocal, osend, orecv = rest
    place = my_place()
    dp, ctx = dp_of(place), ctx_of(place)
    barrier = greet(
        [device_at(dp, lax.rem(ctx + k, N_CTX)) for k in range(1, N_CTX)]
        + [device_at(lax.rem(dp + k, N_DP), ctx) for k in range(1, N_DP)]
    )
    o_ctx = 2 * dp + lax.div(ctx, 8)
    o_home = lax.div(ctx, 2)
    from_ctx = 8 * lax.rem(ctx, 2)
    o_self = o_ctx == ctx
    for t in range(8):
        here = jnp.logical_and(o_home == dp, from_ctx + t == ctx)

        @pl.when(jnp.logical_not(here))
        def _():
            pl.semaphore_signal(
                barrier, inc=1, device_id=device_at(o_home, from_ctx + t), device_id_type=MESH_ID
            )

    pl.semaphore_wait(barrier, 30 - jnp.where(o_self, 1, 0))

    first = []
    for k in range(1, N_CTX):
        to = lax.rem(ctx + k, N_CTX)
        first.append(
            remote(w_ref.at[to], w_out.at[dp, ctx], wsend.at[k], wrecv.at[k], device_at(dp, to))
        )
    for copy in first:
        copy.start()
    own = pltpu.make_async_copy(w_ref.at[ctx], w_out.at[dp, ctx], wlocal)
    own.start()
    rows = RowGather(place, x_ref, x_out, *row_sems)
    rows.start()
    slot = lax.rem(ctx, 8)
    o_own = pltpu.make_async_copy(o_ref, o_out.at[slot], olocal)

    def o_copy(k):
        return remote(o_ref, o_out.at[slot], osend.at[k], orecv.at[slot], device_at(k, o_ctx))

    for k in range(8):
        here = jnp.logical_and(o_self, dp == k)

        @pl.when(here)
        def _():
            o_own.start()

        @pl.when(jnp.logical_not(here))
        def _():
            o_copy(k).start()

    own.wait()
    for copy in first:
        copy.wait_recv()
    second = []
    for k in range(1, N_DP):
        to = lax.rem(dp + k, N_DP)
        second.append(remote(w_out.at[dp], w_out.at[dp], psend.at[k], precv.at[k], device_at(to, ctx)))
    for copy in second:
        copy.start()
    rows.pass_on()
    rows.finish()
    for copy in second:
        copy.wait_recv()
    for t in range(8):
        here = jnp.logical_and(o_home == dp, from_ctx + t == ctx)

        @pl.when(jnp.logical_not(here))
        def _():
            remote(o_ref, o_out.at[t], osend.at[0], orecv.at[t], device_at(dp, ctx)).wait_recv()

    for k in range(8):
        here = jnp.logical_and(o_self, dp == k)

        @pl.when(here)
        def _():
            o_own.wait()

        @pl.when(jnp.logical_not(here))
        def _():
            o_copy(k).wait_send()

    for copy in first + second:
        copy.wait_send()


def entry(x, w, o, number):
    return pl.pallas_call(
        entry_kernel,
        out_shape=(
            jax.ShapeDtypeStruct((N_CTX,) + x.shape, x.dtype),
            jax.ShapeDtypeStruct((N_DP,) + w.shape, w.dtype),
            jax.ShapeDtypeStruct((8,) + o.shape, o.dtype),
        ),
        in_specs=[ANY] * 3,
        out_specs=(ANY, ANY, ANY),
        scratch_shapes=RowGather.scratch
        + [DMA, DMA((16,)), DMA((16,)), DMA((8,)), DMA((8,)), DMA, DMA((8,)), DMA((8,))],
        compiler_params=pltpu.CompilerParams(collective_id=number, has_side_effects=True),
        name="entry_gather",
    )(x, w, o)


def grads_kernel(
    a_ref, b_ref, a_out, b_out, landed, part, wlocal, wsend, wrecv, psend, precv, olocal, osend, orecv, plocal
):
    place = my_place()
    dp, ctx = dp_of(place), ctx_of(place)
    barrier = greet(
        [device_at(dp, lax.rem(ctx + k, N_CTX)) for k in range(1, N_CTX)]
        + [device_at(lax.rem(dp + k, N_DP), ctx) for k in range(1, N_DP)]
    )
    o_ctx = 2 * dp + lax.div(ctx, 8)
    o_home = lax.div(ctx, 2)
    to_ctx = 8 * lax.rem(ctx, 2)
    o_self = o_ctx == ctx
    for k in range(8):
        here = jnp.logical_and(o_self, dp == k)

        @pl.when(jnp.logical_not(here))
        def _():
            pl.semaphore_signal(barrier, inc=1, device_id=device_at(k, o_ctx), device_id_type=MESH_ID)

    pl.semaphore_wait(barrier, 30 - jnp.where(o_self, 1, 0))

    first = []
    for k in range(1, N_DP):
        to = lax.rem(dp + k, N_DP)
        first.append(remote(a_ref.at[to], landed.at[k], wsend.at[k], wrecv.at[k], device_at(to, ctx)))
    for copy in first:
        copy.start()
    own = pltpu.make_async_copy(a_ref.at[dp], landed.at[0], wlocal)
    own.start()

    def o_copy(t):
        return remote(
            b_ref.at[t], b_out.at[dp], osend.at[t], orecv.at[dp], device_at(o_home, to_ctx + t)
        )

    o_own = pltpu.make_async_copy(b_ref.at[lax.rem(ctx, 8)], b_out.at[dp], olocal)
    for t in range(8):
        here = jnp.logical_and(o_home == dp, to_ctx + t == ctx)

        @pl.when(here)
        def _():
            o_own.start()

        @pl.when(jnp.logical_not(here))
        def _():
            o_copy(t).start()

    own.wait()
    total = landed[0].astype(f32)
    for copy in first:
        copy.wait_recv()
    for k in range(1, N_DP):
        total = total + landed[k].astype(f32)
    part[...] = total.reshape(part.shape)
    second = []
    for k in range(1, N_CTX):
        to = lax.rem(ctx + k, N_CTX)
        second.append(remote(part.at[to], a_out.at[ctx], psend.at[k], precv.at[k], device_at(dp, to)))
    for copy in second:
        copy.start()
    mine = pltpu.make_async_copy(part.at[ctx], a_out.at[ctx], plocal)
    mine.start()
    mine.wait()
    for copy in second:
        copy.wait_recv()
    for k in range(8):
        here = jnp.logical_and(o_self, dp == k)

        @pl.when(here)
        def _():
            o_own.wait()

        @pl.when(jnp.logical_not(here))
        def _():
            remote(b_ref.at[0], b_out.at[k], osend.at[0], orecv.at[k], device_at(dp, ctx)).wait_recv()

    for t in range(8):
        here = jnp.logical_and(o_home == dp, to_ctx + t == ctx)

        @pl.when(jnp.logical_not(here))
        def _():
            o_copy(t).wait_send()

    for copy in first + second:
        copy.wait_send()


def grads_out(a, b, number):
    width = a.shape[-1]
    return pl.pallas_call(
        grads_kernel,
        out_shape=(
            jax.ShapeDtypeStruct((N_CTX, 8, width), f32),
            jax.ShapeDtypeStruct((N_DP,) + b.shape[1:], f32),
        ),
        in_specs=[ANY] * 2,
        out_specs=(VMEM, VMEM),
        scratch_shapes=[pltpu.VMEM(a.shape, a.dtype), pltpu.VMEM((N_CTX, 8, width), f32)]
        + [DMA, DMA((8,)), DMA((8,)), DMA((16,)), DMA((16,)), DMA, DMA((8,)), DMA((8,)), DMA],
        compiler_params=pltpu.CompilerParams(
            collective_id=number, has_side_effects=True, vmem_limit_bytes=24 * 2**20
        ),
        name="sum_grads",
    )(a, b)


def swap_halves(u):
    lane = lax.broadcasted_iota(jnp.int32, u.shape, 1)
    return jnp.where(lax.rem(lane, 64) < 32, pltpu.roll(u, 96, 1), pltpu.roll(u, 32, 1))


def attend_kernel(src, order, raw_ref, cos_ref, sin_ref, o_ref, q_ref, k_ref, v_ref, lse_ref, out_nat):
    for b in range(SEQ // BLOCK):
        rows = pl.ds(pl.multiple_of(src[b] * BLOCK, BLOCK), BLOCK)
        here = pl.ds(b * BLOCK, BLOCK)
        qk = raw_ref[rows, 0:128]
        qk = qk * cos_ref[here, :] + swap_halves(qk) * sin_ref[here, :]
        q_ref[here, :] = (qk[:, 0:64]).astype(bf16)
        k_ref[here, :] = (qk[:, 64:128]).astype(bf16)
        v_ref[here, :] = raw_ref[rows, 128:192].astype(bf16)
    step = 256
    for i in range(SEQ // step):
        length = (i + 1) * step
        here = pl.ds(i * step, step)
        scores = dot_last(q_ref[here, :], k_ref[0:length, :]) * 0.125
        row = i * step + lax.broadcasted_iota(jnp.int32, (step, length), 0)
        column = lax.broadcasted_iota(jnp.int32, (step, length), 1)
        scores = jnp.where(column <= row, scores, -1e30)
        top = jnp.max(scores, axis=1, keepdims=True)
        weights = jnp.exp(scores - top)
        total = jnp.sum(weights, axis=1, keepdims=True)
        lse_ref[here, :] = top + jnp.log(total)
        probs = (weights * (1.0 / total)).astype(bf16)
        out_nat[here, :] = dot(probs, v_ref[0:length, :])
    for b in range(SEQ // BLOCK):
        rows = pl.ds(pl.multiple_of(order[b] * BLOCK, BLOCK), BLOCK)
        o_ref[pl.ds(b * BLOCK, BLOCK), :] = out_nat[rows, :].astype(bf16)


def attend(src, order, raw, cosine, sine):
    head = jax.ShapeDtypeStruct((SEQ, HEAD_DIM), bf16)
    return pl.pallas_call(
        attend_kernel,
        out_shape=(head, head, head, head, jax.ShapeDtypeStruct((SEQ, 1), f32)),
        in_specs=[SMEM, SMEM, VMEM, VMEM, VMEM],
        out_specs=(VMEM,) * 5,
        scratch_shapes=[pltpu.VMEM((SEQ, HEAD_DIM), f32)],
        compiler_params=pltpu.CompilerParams(vmem_limit_bytes=48 * 2**20),
        cost_estimate=pl.CostEstimate(flops=10**9, bytes_accessed=6 * 2**20, transcendentals=2**21),
        name="attention_forward",
    )(src, order, raw, cosine, sine)


def attend_back_kernel(
    src, order, q_ref, k_ref, v_ref, lse_ref, do_ref, cos_ref, sin_ref, out_ref, do_nat, acc, done
):
    for b in range(SEQ // BLOCK):
        rows = pl.ds(pl.multiple_of(src[b] * BLOCK, BLOCK), BLOCK)
        do_nat[pl.ds(b * BLOCK, BLOCK), :] = do_ref[rows, :]
    acc[...] = jnp.zeros_like(acc)
    step = 256
    for i in range(SEQ // step):
        length = (i + 1) * step
        here = pl.ds(i * step, step)
        query, d_out = q_ref[here, :], do_nat[here, :].astype(bf16)
        keys = k_ref[0:length, :]
        scores = dot_last(query, keys) * 0.125
        row = i * step + lax.broadcasted_iota(jnp.int32, (step, length), 0)
        column = lax.broadcasted_iota(jnp.int32, (step, length), 1)
        probs = jnp.where(column <= row, jnp.exp(scores - lse_ref[here, :]), 0.0)
        d_probs = dot_last(d_out, v_ref[0:length, :])
        delta = jnp.sum(probs * d_probs, axis=1, keepdims=True)
        d_scores = (probs * (d_probs - delta)).astype(bf16)
        acc[here, 0:64] = dot(d_scores, keys) * 0.125
        acc[0:length, 64:128] += dot_first(d_scores, query) * 0.125
        acc[0:length, 128:192] += dot_first(probs.astype(bf16), d_out)
    for b in range(SEQ // BLOCK):
        here = pl.ds(b * BLOCK, BLOCK)
        qk = acc[here, 0:128]
        qk = qk * cos_ref[here, :] - swap_halves(qk) * sin_ref[here, :]
        done[here, 0:128] = qk
        done[here, 128:256] = acc[here, 128:256]
    for b in range(SEQ // BLOCK):
        rows = pl.ds(pl.multiple_of(order[b] * BLOCK, BLOCK), BLOCK)
        out_ref[pl.ds(b * BLOCK, BLOCK), :] = done[rows, :].astype(bf16)


def attend_back(src, order, q, k, v, lse, d_out, cosine, sine):
    return pl.pallas_call(
        attend_back_kernel,
        out_shape=jax.ShapeDtypeStruct((SEQ, 256), bf16),
        in_specs=[SMEM, SMEM] + [VMEM] * 7,
        out_specs=VMEM,
        scratch_shapes=[
            pltpu.VMEM((SEQ, HEAD_DIM), f32),
            pltpu.VMEM((SEQ, 256), f32),
            pltpu.VMEM((SEQ, 256), f32),
        ],
        compiler_params=pltpu.CompilerParams(vmem_limit_bytes=56 * 2**20),
        cost_estimate=pl.CostEstimate(flops=3 * 10**9, bytes_accessed=6 * 2**20, transcendentals=2**21),
        name="attention_backward",
    )(src, order, q, k, v, lse, d_out, cosine, sine)


def rotary_tables():
    inverse = 10000.0 ** (-np.arange(32, dtype=np.float64) * 2.0 / HEAD_DIM)
    angles = np.arange(SEQ, dtype=np.float64)[:, None] * inverse[None, :]
    cosine, sine = np.cos(angles), np.sin(angles)
    return (
        np.tile(cosine, (1, 4)).astype(np.float32),
        np.concatenate([-sine, sine, -sine, sine], axis=1).astype(np.float32),
    )


def normalize(inputs, gain_values):
    scale_rows = lax.rsqrt(jnp.mean(inputs * inputs, axis=-1, keepdims=True) + epsilon)
    normed = inputs * scale_rows
    return (scale_rows, normed, (normed * gain_values.astype(f32)).astype(bf16))


def norm_backward(grad_in, normed, scale_rows, gain_values):
    grad_normed = grad_in * gain_values.astype(f32)
    inner = jnp.mean(grad_normed * normed, axis=-1, keepdims=True)
    return (scale_rows * (grad_normed - normed * inner), jnp.sum(grad_in * normed, axis=0))


def halves(value):
    high = lax.reduce_precision(value, 8, 7)
    return high.astype(bf16), (value - high).astype(bf16)


def local(
    tokens,
    cotangent,
    block_order,
    routes,
    norm_one,
    w_query,
    w_key,
    w_value,
    w_out,
    norm_two,
    w_router,
    expert_in,
    expert_out,
):
    ctx = lax.axis_index(CTX)
    cosine, sine = (jnp.asarray(t) for t in rotary_tables())
    order = jnp.stack([block_order, 2 * N_CTX - 1 - block_order], axis=1).reshape(-1)
    spots = jnp.arange(2 * N_CTX, dtype=jnp.int32)
    src = jnp.sum(jnp.where(order[None, :] == spots[:, None], spots[None, :], 0), axis=1)

    by_head = lambda w, heads: jnp.moveaxis(w.reshape(8, heads, HEAD_DIM), 1, 0)
    query_part = by_head(w_query, HEADS)
    key_part = jnp.repeat(by_head(w_key, KV_HEADS), 2, axis=0)
    value_part = jnp.repeat(by_head(w_value, KV_HEADS), 2, axis=0)
    small = jnp.concatenate(
        [w_router, norm_one[:, None], norm_two[:, None], jnp.zeros((8, 30), bf16)], axis=1
    )
    small = jnp.broadcast_to(small[None], (N_CTX, 8, 64))
    packed = jnp.concatenate(
        [
            jnp.concatenate([query_part, key_part], axis=2),
            jnp.concatenate([value_part, small], axis=2),
        ],
        axis=1,
    )
    tokens_all, packed_all, out_all = entry(tokens, packed, w_out.reshape(16, 512), 0)
    expert_in_all = lax.all_gather(expert_in, DP, axis=0)
    expert_out_all = lax.all_gather(expert_out, DP, axis=0)
    cotangent_all = lax.all_gather(cotangent, CTX, axis=0)
    low = packed_all[:, :, 8:, :].reshape(D, 128)
    weight = jnp.concatenate(
        [packed_all[:, :, :8, :].reshape(D, 128), low[:, :64], jnp.zeros((D, 64), bf16)], axis=1
    )
    router_weight, gain_one, gain_two = low[:, 64:96], low[:, 96], low[:, 97]
    out_weight = out_all.reshape(HEAD_DIM, D)

    tokens_float = tokens.astype(f32)
    scale_one, normed_one, _ = normalize(tokens_float, gain_one)
    _, _, hidden_one = normalize(tokens_all.reshape(SEQ, D).astype(f32), gain_one)
    raw = dot(hidden_one, weight)
    attended, query, key, value, lse = attend(src, order, raw, cosine, sine)
    partial = dot(attended, out_weight).astype(bf16).reshape(N_CTX, ROWS, D)
    residual = tokens_float + scatter_ctx(partial, 1)
    scale_two, normed_two, hidden_two = normalize(residual, gain_two)

    logits = dot(hidden_two, router_weight)
    names = jnp.arange(EXPERTS, dtype=jnp.int32)
    member = jnp.any(routes[:, :, None] == names[None, None, :], axis=1)
    picked = jnp.where(member, logits, -1e30)
    shifted = jnp.where(member, jnp.exp(picked - jnp.max(picked, axis=1, keepdims=True)), 0.0)
    gates = shifted / jnp.sum(shifted, axis=1, keepdims=True)
    high, rest = halves(gates)
    sent = jnp.concatenate(
        [hidden_two, high, rest, member.astype(bf16), jnp.zeros((ROWS, EXTRA - 96), bf16)], axis=1
    )
    all_two = gather_ctx(sent, 2)

    hidden_all = all_two[:, :, :D]
    pair = lambda at: lax.dynamic_slice_in_dim(all_two, D + at + 2 * ctx, 2, axis=2)
    gate_all = pair(0).astype(f32) + pair(32).astype(f32)
    member_all = pair(64)
    triangle = jnp.tril(jnp.ones((ROWS, ROWS), bf16), -1)
    slot = jnp.einsum("rt,cte->cer", triangle, member_all, preferred_element_type=f32)
    turned = jnp.moveaxis(member_all, 2, 1)
    onehot = jnp.where(
        slot[:, :, None, :] == jnp.arange(MOST, dtype=f32)[None, None, :, None],
        turned[:, :, None, :],
        jnp.zeros((), bf16),
    )
    expert_rows = jnp.einsum("cesr,crd->ecsd", onehot, hidden_all, preferred_element_type=f32).astype(bf16)
    expert_rows = expert_rows.reshape(2, N_CTX * MOST, D)
    d_rows_top = jnp.einsum("cesr,crd->ecsd", onehot, cotangent_all, preferred_element_type=f32)
    d_rows_top = d_rows_top.reshape(2, N_CTX * MOST, D)
    gate_slot = jnp.einsum("cesr,cre->ecs", onehot.astype(f32), gate_all, precision="highest")
    gate_slot = gate_slot.reshape(2, N_CTX * MOST, 1)
    in_weight = jnp.moveaxis(expert_in_all, 0, 1).reshape(2, D, 2 * FF)
    down_weight = jnp.moveaxis(expert_out_all, 0, 2).reshape(2, FF, D)
    gate_up = jnp.einsum("esd,edf->esf", expert_rows, in_weight, preferred_element_type=f32)
    gate_part, up_part = gate_up[..., :FF], gate_up[..., FF:]
    expert_hidden = (jax.nn.silu(gate_part) * up_part).astype(bf16)
    expert_result = jnp.einsum("esf,efd->esd", expert_hidden, down_weight, preferred_element_type=f32)
    expert_result = expert_result.astype(bf16).astype(f32)
    d_gate_slot = jnp.sum(d_rows_top * expert_result, axis=-1)
    weighted = (expert_result * gate_slot).astype(bf16).reshape(2, N_CTX, MOST, D)
    out_part = jnp.einsum("cesr,ecsd->crd", onehot, weighted, preferred_element_type=f32).astype(bf16)
    output = residual + scatter_ctx(out_part, 3)
    d_result = (d_rows_top * gate_slot).astype(bf16)
    d_hidden = jnp.einsum("esd,efd->esf", d_result, down_weight, preferred_element_type=f32)
    grad_down = jnp.einsum("esf,esd->efd", expert_hidden, d_result, preferred_element_type=f32)
    sigmoid_gate = jax.nn.sigmoid(gate_part)
    d_gate = d_hidden * up_part * (sigmoid_gate * (1.0 + gate_part * (1.0 - sigmoid_gate)))
    d_up = d_hidden * jax.nn.silu(gate_part)
    d_gate_up = jnp.concatenate([d_gate, d_up], axis=-1).astype(bf16)
    grad_in = jnp.einsum("esd,esf->edf", expert_rows, d_gate_up, preferred_element_type=f32)
    d_rows = jnp.einsum("esf,edf->esd", d_gate_up, in_weight, preferred_element_type=f32).astype(bf16)
    d_part = jnp.einsum(
        "cesr,ecsd->crd", onehot, d_rows.reshape(2, N_CTX, MOST, D), preferred_element_type=f32
    ).astype(bf16)
    d_gate_rows = jnp.sum(
        onehot.astype(f32) * jnp.moveaxis(d_gate_slot.reshape(2, N_CTX, MOST), 0, 1)[..., None], axis=2
    )
    dg_high, dg_rest = halves(jnp.moveaxis(d_gate_rows, 1, 2))
    put = lambda v: lax.dynamic_update_slice_in_dim(
        jnp.zeros((N_CTX, ROWS, EXPERTS), bf16), v, 2 * ctx, axis=2
    )
    d_part = jnp.concatenate(
        [d_part, put(dg_high), put(dg_rest), jnp.zeros((N_CTX, ROWS, EXTRA - 64), bf16)], axis=2
    )
    grad_in = lax.psum_scatter(
        jnp.moveaxis(grad_in.reshape(2, N_DP, ROWS, 2 * FF), 1, 0).astype(bf16), DP, scatter_dimension=0
    ).astype(f32)
    grad_down = lax.psum_scatter(
        jnp.moveaxis(grad_down.reshape(2, FF, N_DP, ROWS), 2, 0).astype(bf16), DP, scatter_dimension=0
    ).astype(f32)
    d_sum = scatter_ctx(d_part, 4)

    grad_top = cotangent.astype(f32)
    d_gates = d_sum[:, D : D + 32] + d_sum[:, D + 32 : D + 64]
    d_picked = gates * (d_gates - jnp.sum(gates * d_gates, axis=1, keepdims=True))
    d_logits = d_picked.astype(bf16)
    d_hidden_two = d_sum[:, :D] + dot_last(d_logits, router_weight)
    d_norm_two, grad_gain_two = norm_backward(d_hidden_two, normed_two, scale_two, gain_two)
    d_residual = grad_top + d_norm_two
    sent = jnp.concatenate(
        [d_residual.astype(bf16), d_logits, jnp.zeros((ROWS, EXTRA - 32), bf16)], axis=1
    )
    all_three = gather_ctx(sent, 5).reshape(SEQ, D + EXTRA)
    d_branch = all_three[:, :D]
    d_logits_all = all_three[:, D : D + 32]

    d_attended = dot_last(d_branch, out_weight).astype(bf16).astype(f32)
    d_raw = attend_back(src, order, query, key, value, lse, d_attended, cosine, sine)
    d_one = dot_last(d_raw, weight).astype(bf16).reshape(N_CTX, ROWS, D)
    d_hidden_one = scatter_ctx(d_one, 6)
    d_norm_one, grad_gain_one = norm_backward(d_hidden_one, normed_one, scale_one, gain_one)
    input_grad = d_residual + d_norm_one

    grad_out_weight = dot_first(attended, d_branch)
    own_columns = lax.dynamic_slice_in_dim(hidden_all.reshape(SEQ, D), ctx * 64, 64, axis=1)
    grad_router = dot_first(own_columns, d_logits_all)
    second = jnp.concatenate(
        [grad_out_weight, grad_router, jnp.zeros((64, EXTRA - 32), f32)], axis=1
    ).reshape(8, 8, D + EXTRA)
    grad_heads = dot_first(hidden_one, d_raw)
    first = jnp.concatenate(
        [
            grad_heads[:, :192],
            grad_gain_one[:, None],
            grad_gain_two[:, None],
            jnp.zeros((D, 62), f32),
        ],
        axis=1,
    ).astype(bf16)
    a, b = grads_out(first.reshape(N_DP, ROWS, 256), second, 7)
    b = jnp.sum(b, axis=0)
    side = lambda v: jnp.moveaxis(v, 0, 1).reshape(8, -1)
    pairs = a.reshape(KV_HEADS, 2, 8, 256).sum(axis=1)
    gains = jnp.sum(a[:, :, 192:194], axis=0)
    return (
        output,
        input_grad,
        gains[:, 0],
        side(a[:, :, 0:64]),
        side(pairs[:, :, 64:128]),
        side(pairs[:, :, 128:192]),
        b[:, :D],
        gains[:, 1],
        b[:, D : D + 32],
        grad_in,
        grad_down,
    )


def solution(mesh):
    split = Mesh(mesh.devices.reshape(2, 4, 2, 4, 2), AXES)
    rows = P(AXES, None)
    line = P(AXES)
    return jax.shard_map(
        local,
        mesh=split,
        in_specs=(
            rows,
            rows,
            P(),
            rows,
            line,
            rows,
            rows,
            rows,
            rows,
            line,
            rows,
            P(CTX, DP, None),
            P(CTX, None, DP),
        ),
        out_specs=(
            rows,
            rows,
            line,
            rows,
            rows,
            rows,
            rows,
            line,
            rows,
            P(CTX, DP, None),
            P(CTX, None, DP),
        ),
        check_vma=False,
    )
```

time: 1500 us -> 551 us (0.37)
  waiting for transfers between devices: 1040 us -> 36.3 us
  Pallas kernels: 0 us -> 332 us
  local copies, waits for them, and re-layouts: 162 us -> 72.3 us
  matrix products: 144 us -> 60.6 us
  blocking collectives: 45.9 us -> 0 us
  other arithmetic: 58.6 us -> 23.4 us
  starting transfers between devices: 15.9 us -> 0.19 us
    unnamed x11 -> x5, waiting for transfers between devices: 709 us -> 2.09 us
    pallas_call x0 -> x10, Pallas kernels: none -> 332 us  [the longest x4 148 us: scatter_ctx(): pl.pallas_call(scatter_kernel, out_shape=jax.ShapeDtypeStruct((rows, widt...]
    all_gather x3, waiting for transfers between devices: 232 us -> 34.2 us  [the longest x1 34.2 us: local(): cotangent_all = lax.all_gather(cotangent, CTX, axis=0)]
    all_to_all x3 -> x0, waiting for transfers between devices: 98.8 us -> none  [the longest x1 38.5 us: local(): lax.all_to_all(expert_result, 'ctx', split_axis=0, concat_axis=0, tiled=T...]
    dot_general x57 -> x21, matrix products: 144 us -> 60.6 us  [the longest x3 8.55 us: dot_first(): lax.dot_general(a, b, (((0,), (0,)), ((), ())), preferred_element_type=f32)]
    all_to_all x1 -> x0, blocking collectives: 45.9 us -> none  [local(): lax.all_to_all(d_send, 'ctx', split_axis=0, concat_axis=0, tiled=True)]
    reshape x15 -> x11, local copies, waits for them, and re-layouts: 37.6 us -> 10.4 us  [the longest x1 4.53 us: local(): down_weight = jnp.moveaxis(expert_out_all, 0, 2).reshape(2, FF, D)]
    gather x4 -> x0, local copies, waits for them, and re-layouts: 22.3 us -> none  [the longest x1 5.86 us: local(): taken = jnp.take(hidden_two, slot_source // TOP, axis=0)]
  transfers between devices with their start and end apart: 12 -> 5, of which waited for: 7 -> 1; matrix products, arithmetic and copies ran while one was open for 21% -> 25% of each run, Pallas kernels for 0% -> 61%
where the time goes in v1:
time: 551 us; the launch traced here: 540 us
  Pallas kernels  332 us (60%)
  local copies, waits for them, and re-layouts  72.3 us (13%)
  matrix products  60.6 us (11%)
  waiting for transfers between devices  36.3 us (7%)
  other arithmetic  23.4 us (4%)
  between operations  15.2 us (3%)
    pallas_call x4, Pallas kernels, scatter_ctx(): pl.pallas_call(scatter_kernel, out_shape=jax.ShapeDtypeStruct((rows, widt...  148 us
    pallas_call x2, Pallas kernels, gather_ctx(): pl.pallas_call(gather_kernel, out_shape=jax.ShapeDtypeStruct((N_CTX,) + x...  85.5 us
    pallas_call x1, Pallas kernels, entry(): pl.pallas_call(entry_kernel, out_shape=(jax.ShapeDtypeStruct((N_CTX,) + x...  53.7 us
    all_gather x1, waiting for transfers between devices, local(): cotangent_all = lax.all_gather(cotangent, CTX, axis=0)  34.2 us
    pallas_call x1, Pallas kernels, grads_out(): pl.pallas_call(grads_kernel, out_shape=(jax.ShapeDtypeStruct((N_CTX, 8, w...  22.2 us
    pallas_call x1, Pallas kernels, attend_back(): pl.pallas_call(attend_back_kernel, out_shape=jax.ShapeDtypeStruct((SEQ, 2...  13.7 us
  transfers between devices with their start and end apart: 5, of which 1 were waited for; matrix products, arithmetic and copies ran while one was open for 25% of the time, Pallas kernels for 61%

profile of v1, /device:TPU:1, one launch (start us, length us, event | category | flops | bytes accessed | tf_op | source)
XLA Modules:
  0.0 540.1 jit_solution(1625194487932143838)
XLA Ops:
  16.6 1.3 reshape.190.o_ref
  18.7 53.7 %entry_gather.1 = (bf16[16,128,1024]{2,1,0:T(8,128)(2,1)}, bf16[8,16,16,128]{3,2,1,0:T(8,128)(2,1)}, bf16[8,16,512]{2,1,0:T(8,128)(2,1)}) custom-call(bf16[128,1024]{1,0:T(8,128)(2,1)} %x_ref.1, bf16[16,16,128]{2,1,0:T(8,128)(2,1)} %maximum_maximum_fusion.4.w_ref, bf16[16,512]{1,0:T(8,128)(2,1)} %reshape.190.o_ref), custom_call_target="tpu_custom_call" | custom-call | tf_op jit(solution)/shard_map/entry_gather/pallas_call | solution.py:312
  74.2 3.2 multiply_reduce_fusion
  78.8 2.6 fusion.42.raw_ref
  81.8 8.7 %attention_forward.1 = (bf16[2048,64]{1,0:T(8,128)(2,1)S(1)}, bf16[2048,64]{1,0:T(8,128)(2,1)S(1)}, bf16[2048,64]{1,0:T(8,128)(2,1)S(1)}, bf16[2048,64]{1,0:T(8,128)(2,1)S(1)}, f32[2048,1]{1,0:T(8,128)S(1)}) custom-call(s32[32]{0:T(128)S(1)} %select_reduce_fusion.src, s32[32]{0:T(128)S(1)} %eq.20.order, f32[2048,256]{1,0:T(8,128)} %fusion.42.raw_ref, ...), custom_call_target="tpu_custom_call" | custom-call | flops 1000000000 | bytes 6291456 | tf_op jit(solution)/shard_map/attention_forward/pallas_call | solution.py:470
  92.0 36.9 %scatter_rows.4 = f32[128,1024]{1,0:T(8,128)S(1)} custom-call(bf16[8,2,128,1024]{3,2,1,0:T(8,128)(2,1)S(1)} %bitcast.141), custom_call_target="tpu_custom_call" | custom-call | tf_op jit(solution)/shard_map/scatter_rows/pallas_call | solution.py:201
  131.7 42.1 %gather_rows.2 = bf16[16,128,1152]{2,1,0:T(8,128)(2,1)} custom-call(bf16[128,1152]{1,0:T(8,128)(2,1)} %concatenate.47.x_ref), custom_call_target="tpu_custom_call" | custom-call | tf_op jit(solution)/shard_map/gather_rows/pallas_call | solution.py:154
  175.5 1.3 fusion.108
  177.0 3.2 convert_bitcast_fusion
  180.2 2.0 copy.202
  182.2 2.6 add_bitcast_fusion
  184.8 1.6 copy.229
  187.2 4.3 copy.257
  191.6 4.5 reshape.196
  196.1 2.8 copy.203
  199.3 3.4 fusion.83
  202.7 2.6 copy-done.11
  205.3 2.2 multiply_convert_fusion.2
  207.5 34.2 %all-gather.11.cloned.1.call-done = bf16[2048,1024]{1,0:T(8,128)(2,1)} async-done(((bf16[128,1024]{1,0:T(8,128)(2,1)}), bf16[2048,1024]{1,0:T(8,128)(2,1)}) %all-gather.11.cloned.1.call-update) | async-done | bytes 4194320 | tf_op jit(solution)/shard_map/all_gather | solution.py:599
  241.7 3.2 convolution_bitcast_fusion
  246.9 3.9 fusion.3
  250.9 1.9 convert_bitcast_fusion.1
  252.8 1.9 copy.256
  254.8 7.5 %multiply_convert_fusion.1 = (bf16[2,768,512]{2,1,0:T(8,128)(2,1)S(1)}, bf16[2,768,512]{2,1,0:T(8,128)(2,1)S(1)}) fusion(f32[2,768,1024]{2,1,0:T(8,128)} %copy-done.11, bf16[2,768,1024]{2,1,0:T(8,128)(2,1)} %copy-done.16, bf16[2,512,1024]{2,1,0:T(8,128)(2,1)} %reshape.196), kind=kOutput, calls=%fused_computation.25 | convolution fusion | flops 1620836352 | bytes 14680064 | tf_op jit(solution)/shard_map/esd,efd->esf/dot_general | solution.py:658
  262.3 4.0 convolution_convert_fusion.2
  266.2 2.5 copy.255
  268.8 4.9 slice.76
  275.5 5.1 dynamic_update_slice.6
  280.7 5.1 dynamic_update_slice.7
  285.8 6.6 %convolution_convert_fusion.4 = bf16[2,768,1024]{2,1,0:T(8,128)(2,1)S(1)} fusion(bf16[2,1024,1024]{2,1,0:T(8,128)(2,1)} %bitcast.162, bf16[2,768,512]{2,1,0:T(8,128)(2,1)} %copy-done.43, bf16[2,768,512]{2,1,0:T(8,128)(2,1)} %copy-done.42), kind=kOutput, calls=%fused_computation.34 | convolution fusion | flops 3229089792 | bytes 10485760 | tf_op jit(solution)/shard_map/esf,edf->esd/dot_general | solution.py:665
  292.4 3.4 bitcast_convert_fusion
  295.9 8.4 %concatenate.49 = bf16[16,128,1152]{2,1,0:T(8,128)(2,1)} concatenate(bf16[16,128,1024]{2,1,0:T(8,128)(2,1)} %bitcast_convert_fusion, bf16[16,128,32]{2,1,0:T(8,128)(2,1)S(1)} %dynamic_update_slice.6, bf16[16,128,32]{2,1,0:T(8,128)(2,1)S(1)} %dynamic_update_slice.7, bf16[16,128,64]{2,1,0:T(8,128)(2,1)S(1)} %broadcast_in_dim.115), dimensions={2} | concatenate | bytes 9437184 | tf_op jit(solution)/shard_map/concatenate | solution.py:676
  304.3 2.7 copy-done
  307.1 40.0 %scatter_rows.6 = f32[128,1152]{1,0:T(8,128)S(1)} custom-call(bf16[8,2,128,1152]{3,2,1,0:T(8,128)(2,1)S(1)} %bitcast.143), custom_call_target="tpu_custom_call" | custom-call | tf_op jit(solution)/shard_map/scatter_rows/pallas_call | solution.py:201
  349.4 43.4 %gather_rows.3 = bf16[16,128,1152]{2,1,0:T(8,128)(2,1)} custom-call(bf16[128,1152]{1,0:T(8,128)(2,1)} %concatenate.50.x_ref), custom_call_target="tpu_custom_call" | custom-call | tf_op jit(solution)/shard_map/gather_rows/pallas_call | solution.py:154
  392.9 3.6 fusion.14
  397.8 13.7 %attention_backward.1 = bf16[2048,256]{1,0:T(8,128)(2,1)} custom-call(s32[32]{0:T(128)} %copy-done.4, s32[32]{0:T(128)} %copy-done.3, bf16[2048,64]{1,0:T(8,128)(2,1)} %copy-done.6, bf16[2048,64]{1,0:T(8,128)(2,1)} %copy-done.7, bf16[2048,64]{1,0:T(8,128)(2,1)} %copy-done.8, f32[2048,1]{1,0:T(8,128)} %copy-done.5, f32[2048,64]{1,0:T(8,128)} %convert_element_type.182.do_ref, ...), custom_call_target="tpu_custom_call" | custom-call | flops 3000000000 | bytes 6291456 | tf_op jit(solution)/shard_map/attention_backward/pallas_call | solution.py:517
  411.5 2.5 convolution_convert_fusion
  414.1 35.5 %scatter_rows.7 = f32[128,1024]{1,0:T(8,128)S(1)} custom-call(bf16[8,2,128,1024]{3,2,1,0:T(8,128)(2,1)S(1)} %bitcast.142), custom_call_target="tpu_custom_call" | custom-call | tf_op jit(solution)/shard_map/scatter_rows/pallas_call | solution.py:201
  452.2 3.8 fusion.84
  456.2 1.7 fusion.29
  457.9 3.1 fusion.7
  461.1 1.3 maximum_maximum_fusion.1.a_ref
  462.4 22.2 %sum_grads.1 = (f32[16,8,256]{2,1,0:T(8,128)S(1)}, f32[8,8,1152]{2,1,0:T(8,128)S(1)}) custom-call(bf16[8,128,256]{2,1,0:T(8,128)(2,1)S(1)} %maximum_maximum_fusion.1.a_ref, f32[8,8,1152]{2,1,0:T(8,128)S(1)} %bitcast.145), custom_call_target="tpu_custom_call" | custom-call | tf_op jit(solution)/shard_map/sum_grads/pallas_call | solution.py:418
  485.9 3.2 bitcast_convert_fusion.1
  489.1 35.9 %scatter_rows.5 = f32[128,1024]{1,0:T(8,128)S(1)} custom-call(bf16[8,2,128,1024]{3,2,1,0:T(8,128)(2,1)S(1)} %bitcast.144), custom_call_target="tpu_custom_call" | custom-call | tf_op jit(solution)/shard_map/scatter_rows/pallas_call | solution.py:201
  529.3 1.8 bitcast_convert_fusion.3
  531.0 2.1 bitcast_convert_fusion.2
  (195 shorter events, 36.8 us)
Async XLA Ops:
  7.2 180.1 %all-gather.9.cloned.1.call-start = ((), (), s32[]{:S(2)}) async-start(), calls=%async_computation.5 | async-start | bytes 2359296 | tf_op jit(solution)/shard_map/all_gather | solution.py:598
  7.9 188.2 %all-gather.7.cloned.1.call-start = ((), (), s32[]{:S(2)}) async-start(), calls=%async_computation.4 | async-start | bytes 4718592 | tf_op jit(solution)/shard_map/all_gather | solution.py:597
  8.7 233.0 %all-gather.11.cloned.1.call-start = ((), (), s32[]{:S(2)}) async-start(), calls=%async_computation.6 | async-start | bytes 4456448 | tf_op jit(solution)/shard_map/all_gather | solution.py:599
  9.4 519.9 %reduce-scatter.5.cloned.1.call-start = ((), (), s32[]{:S(2)}) async-start(), calls=%async_computation.3 | async-start | bytes 2359296 | tf_op jit(solution)/shard_map/reduce_scatter | solution.py:682
  11.8 69.6 %copy-start.3 = (s32[32]{0:T(128)}, s32[32]{0:T(128)S(1)}, u32[]{:S(2)}) copy-start(s32[32]{0:T(128)S(1)} %eq.20.order) | copy-start | bytes 388
  72.4 1.6 copy-start.26
  73.5 5.2 copy-start.20
  73.9 4.8 copy-start.29
  74.0 4.8 copy-start.38
  74.1 16.5 %copy-start.22 = (bf16[64,1024]{1,0:T(8,128)(2,1)}, bf16[64,1024]{1,0:T(8,128)(2,1)S(1)}, u32[]{:S(2)}) copy-start(bf16[64,1024]{1,0:T(8,128)(2,1)S(1)} %reshape.193) | copy-start | bytes 393220
  74.1 3.5 copy-start.9
  74.2 7.2 %copy-start.4 = (s32[32]{0:T(128)}, s32[32]{0:T(128)S(1)}, u32[]{:S(2)}) copy-start(s32[32]{0:T(128)S(1)} %select_reduce_fusion.src) | copy-start | bytes 388
  78.7 2.8 copy-start.13
  78.8 2.8 copy-start.1
  78.8 3.1 copy-start.2
  90.6 1.3 copy-start.5
  90.6 1.3 copy-start.6
  90.6 1.3 copy-start.7
  90.6 1.4 copy-start.8
  92.0 37.2 %copy-start.15 = (bf16[128,1024]{1,0:T(8,128)(2,1)S(1)}, bf16[128,1024]{1,0:T(8,128)(2,1)}, u32[]{:S(2)}) copy-start(bf16[128,1024]{1,0:T(8,128)(2,1)} %x_ref.1) | copy-start | bytes 786436
  129.1 218.8 %copy-start.27 = (f32[1024,1]{0,1:T(1,128)}, f32[1024,1]{0,1:T(1,128)S(1)}, u32[]{:S(2)}) copy-start(f32[1024,1]{0,1:T(1,128)S(1)} %copy.242) | copy-start | bytes 12292
  130.0 217.9 %copy-start.32 = (f32[128]{0:T(128)}, f32[128]{0:T(128)S(1)}, u32[]{:S(2)}) copy-start(f32[128]{0:T(128)S(1)} %get-tuple-element.61) | copy-start | bytes 1540
  177.0 115.4 %copy-start.24 = (bf16[16,2,128]{2,1,0:T(2,128)(2,1)}, bf16[16,2,128]{2,1,0:T(2,128)(2,1)S(1)}, u32[]{:S(2)}) copy-start(bf16[16,2,128]{2,1,0:T(2,128)(2,1)S(1)} %copy.201) | copy-start | bytes 24580
  196.1 3.2 copy-start.17
  198.9 3.8 copy-start.14
  202.7 2.6 copy-start.11
  244.9 1.6 copy-start.10
  244.9 2.0 copy-start.12
  250.9 1.9 copy-start.16
  254.7 276.3 %reduce-scatter.3.cloned.1.call-start = ((), (), s32[]{:S(2)}) async-start(), calls=%async_computation.2 | async-start | bytes 4718592 | tf_op jit(solution)/shard_map/reduce_scatter | solution.py:679
  254.8 7.5 %copy-start.18 = (bf16[2,16,48,1024]{3,2,1,0:T(8,128)(2,1)S(1)}, bf16[2,16,48,1024]{3,2,1,0:T(8,128)(2,1)}, u32[]{:S(2)}) copy-start(bf16[2,16,48,1024]{3,2,1,0:T(8,128)(2,1)} %copy.202) | copy-start | bytes 9437188
  262.2 4.0 copy-start.42
  262.2 4.0 copy-start.43
  304.3 2.7 copy-start
  307.1 41.3 %copy-start.19 = (bf16[128,1024]{1,0:T(8,128)(2,1)S(1)}, bf16[128,1024]{1,0:T(8,128)(2,1)}, u32[]{:S(2)}) copy-start(bf16[128,1024]{1,0:T(8,128)(2,1)} %param.16) | copy-start | bytes 786436
  348.6 44.3 %copy-start.23 = (bf16[64,1024]{1,0:T(8,128)(2,1)S(1)}, bf16[64,1024]{1,0:T(8,128)(2,1)}, u32[]{:S(2)}) copy-start(bf16[64,1024]{1,0:T(8,128)(2,1)} %copy-done.22) | copy-start | bytes 393220
  397.8 13.7 %copy-start.21 = (bf16[8,16,8,128]{3,2,1,0:T(8,128)(2,1)S(1)}, bf16[8,16,8,128]{3,2,1,0:T(8,128)(2,1)}, u32[]{:S(2)}) copy-start(bf16[8,16,8,128]{3,2,1,0:T(8,128)(2,1)} %copy-done.20) | copy-start | bytes 786436
  397.8 13.7 %copy-start.39 = (bf16[256]{0:T(256)(128)(2,1)S(1)}, bf16[256]{0:T(256)(128)(2,1)}, u32[]{:S(2)}) copy-start(bf16[256]{0:T(256)(128)(2,1)} %copy-done.38) | copy-start | bytes 1540
  414.1 36.4 %copy-start.30 = (f32[1024,1]{0,1:T(1,128)S(1)}, f32[1024,1]{0,1:T(1,128)}, u32[]{:S(2)}) copy-start(f32[1024,1]{0,1:T(1,128)} %copy-done.29) | copy-start | bytes 12292
  414.1 36.4 %copy-start.34 = (f32[128]{0:T(128)S(1)}, f32[128]{0:T(128)}, u32[]{:S(2)}) copy-start(f32[128]{0:T(128)} %get-tuple-element.60) | copy-start | bytes 1540
  456.2 4.9 copy-start.40
  457.9 27.9 %copy-start.25 = (bf16[16,2,128]{2,1,0:T(2,128)(2,1)S(1)}, bf16[16,2,128]{2,1,0:T(2,128)(2,1)}, u32[]{:S(2)}) copy-start(bf16[16,2,128]{2,1,0:T(2,128)(2,1)} %copy-done.24) | copy-start | bytes 24580
  489.1 38.9 %copy-start.41 = (f32[128]{0:T(128)S(1)}, f32[128]{0:T(128)}, u32[]{:S(2)}) copy-start(f32[128]{0:T(128)} %get-tuple-element.34) | copy-start | bytes 1540
  489.1 38.9 %copy-start.28 = (f32[1024,1]{0,1:T(1,128)S(1)}, f32[1024,1]{0,1:T(1,128)}, u32[]{:S(2)}) copy-start(f32[1024,1]{0,1:T(1,128)} %copy-done.27) | copy-start | bytes 12292
  489.1 38.9 %copy-start.31 = (f32[1024,1]{0,1:T(1,128)S(1)}, f32[1024,1]{0,1:T(1,128)}, u32[]{:S(2)}) copy-start(f32[1024,1]{0,1:T(1,128)} %copy-done.29) | copy-start | bytes 12292
  489.1 38.9 %copy-start.33 = (f32[128]{0:T(128)S(1)}, f32[128]{0:T(128)}, u32[]{:S(2)}) copy-start(f32[128]{0:T(128)} %copy-done.32) | copy-start | bytes 1540
  489.1 38.9 %copy-start.35 = (f32[128]{0:T(128)S(1)}, f32[128]{0:T(128)}, u32[]{:S(2)}) copy-start(f32[128]{0:T(128)} %get-tuple-element.60) | copy-start | bytes 1540
  489.1 38.9 %copy-start.37 = (f32[128]{0:T(128)S(1)}, f32[128]{0:T(128)}, u32[]{:S(2)}) copy-start(f32[128]{0:T(128)} %copy-done.36) | copy-start | bytes 1540
  (1 other events, 0.5 us)
Sparse Core Ops, SparseCore 0:
  9.7 70.9 all-gather.8
  82.3 101.9 all-gather.6
  186.8 54.9 all-gather.10
  254.8 36.1 reduce-scatter.4
  293.3 107.3 reduce-scatter.2

commit v2 on v1

--- a/solution.py
+++ b/solution.py
@@ -35,7 +35,6 @@
 bf16 = jnp.bfloat16
 f32 = jnp.float32
 epsilon = 1e-06
-CHIPS = [(0, 1), (1, 0), (0, 3), (1, 1), (1, 3), (0, 2), (1, 2)]
 
 
 def dot(a, b):
@@ -64,16 +63,9 @@
     )
 
 
-def chip_peer(place, n):
+def beside(place, dy, dx):
     ylo, z, yhi, x, core = place
-    dy, dx = CHIPS[n]
     return (ylo, z, lax.rem(yhi + dy, 2), lax.rem(x + dx, 4), core)
-
-
-def chip_from(place, n):
-    ylo, z, yhi, x, core = place
-    dy, dx = CHIPS[n]
-    return (ylo, z, lax.rem(yhi + dy, 2), lax.rem(x + 4 - dx, 4), core)
 
 
 def ctx_of(place):
@@ -102,49 +94,71 @@
 
 
 class RowGather:
-    scratch = [DMA, DMA((8,)), DMA((8,)), DMA((7,)), DMA((7,))]
-
-    def __init__(self, place, x_ref, out_ref, local, send, recv, fsend, frecv):
-        me = ctx_of(place)
+    scratch = [DMA, DMA((9,)), DMA((9,)), DMA((10,)), DMA((10,))]
+    links = [(1, 0), (0, 1), (0, 3), (0, 1), (0, 3), (0, 1), (0, 3), (0, 1), (0, 3)]
+    held = [(0, 0), (0, 0), (0, 0), (1, 0), (1, 0), (0, 3), (0, 1), (1, 3), (1, 1)]
+    parts = [None, None, None, None, None, 0, 1, 0, 1]
+    after = {0: (3, 4), 1: (5,), 2: (6,), 3: (7,), 4: (8,)}
+
+    def __init__(self, place, x_ref, view, half, local, send, recv, fsend, frecv):
         sibling = sibling_of(place)
-        self.own = pltpu.make_async_copy(x_ref, out_ref.at[me], local)
-        self.out = [
-            remote(x_ref, out_ref.at[me], send.at[n], recv.at[n], chip_peer(place, n)) for n in range(7)
-        ]
-        self.out.append(remote(x_ref, out_ref.at[me], send.at[7], recv.at[7], sibling))
-        self.forward = []
-        for n in range(7):
-            piece = out_ref.at[ctx_of(chip_from(place, n))]
-            self.forward.append(remote(piece, piece, fsend.at[n], frecv.at[n], sibling))
+
+        def piece(dy, dx, part):
+            ref = view(beside(place, dy, dx))
+            return ref if part is None else ref.at[pl.ds(part * half, half)]
+
+        self.own = pltpu.make_async_copy(x_ref, view(place), local)
+        self.out, self.landed, self.passed = [], [], []
+        for n, ((ly, lx), (hy, hx), part) in enumerate(zip(self.links, self.held, self.parts)):
+            source = x_ref if n < 3 else piece(hy, hx, part)
+            self.out.append(
+                remote(source, piece(hy, hx, part), send.at[n], recv.at[n], beside(place, ly, lx))
+            )
+            here = piece((hy + ly) % 2, (hx + 4 - lx) % 4, part)
+            self.landed.append(remote(here, here, send.at[n], recv.at[n], beside(place, ly, lx)))
+            self.passed.append(remote(here, here, fsend.at[n], frecv.at[n], sibling))
+        self.passed.append(remote(x_ref, view(place), fsend.at[9], frecv.at[9], sibling))
+        self.back = []
+        for n in range(9):
+            (ly, lx), (hy, hx), part = self.links[n], self.held[n], self.parts[n]
+            ref = view(sibling_of(beside(place, (hy + ly) % 2, (hx + 4 - lx) % 4)))
+            ref = ref if part is None else ref.at[pl.ds(part * half, half)]
+            self.back.append(remote(ref, ref, fsend.at[n], frecv.at[n], sibling))
+        ref = view(sibling)
+        self.back.append(remote(ref, ref, fsend.at[9], frecv.at[9], sibling))
 
     def start(self):
-        for copy in self.out:
-            copy.start()
+        for n in range(3):
+            self.out[n].start()
+        self.passed[9].start()
         self.own.start()
 
+    def step(self, n):
+        self.landed[n].wait_recv()
+        for m in self.after.get(n, ()):
+            self.out[m].start()
+        self.passed[n].start()
+
     def pass_on(self):
-        for n in range(7):
-            self.out[n].wait_recv()
-            self.forward[n].start()
+        for n in range(9):
+            self.step(n)
 
     def finish(self):
         self.own.wait()
-        self.out[7].wait_recv()
-        for n in range(7):
-            self.forward[n].wait_recv()
-        for copy in self.out + self.forward:
+        for n in range(10):
+            self.back[n].wait_recv()
+        for copy in self.out + self.passed:
             copy.wait_send()
 
 
-def greet_chips(place):
-    barrier = greet([chip_peer(place, n) for n in range(7)] + [sibling_of(place)])
-    pl.semaphore_wait(barrier, 8)
+def chip_neighbours(place):
+    return [beside(place, 1, 0), beside(place, 0, 1), beside(place, 0, 3), sibling_of(place)]
 
 
 def gather_kernel(x_ref, out_ref, *sems):
     place = my_place()
-    greet_chips(place)
-    gather = RowGather(place, x_ref, out_ref, *sems)
+    pl.semaphore_wait(greet(chip_neighbours(place)), 4)
+    gather = RowGather(place, x_ref, lambda p: out_ref.at[ctx_of(p)], x_ref.shape[0] // 2, *sems)
     gather.start()
     gather.pass_on()
     gather.finish()
@@ -162,37 +176,103 @@
     )(x)
 
 
-def scatter_kernel(p_ref, out_ref, own, other, landed, own_sem, send, recv, csend, crecv):
+SPREAD = [(1, 2), (0, 2), (1, 1), (1, 3), (0, 1), (0, 3), (1, 0), (0, 0)]
+
+
+class RowScatter:
+    @staticmethod
+    def scratch(rows, width):
+        return [
+            pltpu.VMEM((8, rows, width), bf16),
+            pltpu.VMEM((8, rows, width), bf16),
+            pltpu.VMEM((4, rows // 2, width), bf16),
+            pltpu.VMEM((4, rows, width), bf16),
+            pltpu.VMEM((rows, width), bf16),
+            DMA((8,)),
+            DMA((8,)),
+            DMA((8,)),
+            DMA((9,)),
+            DMA((9,)),
+        ]
+
+    def __init__(self, place, p_ref, own, other, halves, wholes, last, own_sem, fsend, frecv, send, recv):
+        self.own, self.other, self.halves, self.wholes, self.last = own, other, halves, wholes, last
+        core = place[4]
+        half = own.shape[1] // 2
+        self.half = half
+        self.mine, self.cross = [], []
+        for n, (dy, dx) in enumerate(SPREAD):
+            chip = lax.div(ctx_of(beside(place, dy, dx)), 2)
+            self.mine.append(pltpu.make_async_copy(p_ref.at[chip, core], own.at[n], own_sem.at[n]))
+            self.cross.append(
+                remote(p_ref.at[chip, 1 - core], other.at[n], fsend.at[n], frecv.at[n], sibling_of(place))
+            )
+        right, left = beside(place, 0, 1), beside(place, 0, 3)
+        self.out = []
+        for n, (source, target, device) in enumerate(
+            [
+                (own.at[0, pl.ds(0, half)], halves.at[0], right),
+                (own.at[0, pl.ds(half, half)], halves.at[1], left),
+                (own.at[1, pl.ds(0, half)], halves.at[2], right),
+                (own.at[1, pl.ds(half, half)], halves.at[3], left),
+                (own.at[2], wholes.at[0], right),
+                (own.at[3], wholes.at[1], left),
+                (own.at[4], wholes.at[2], right),
+                (own.at[5], wholes.at[3], left),
+                (own.at[6], last, beside(place, 1, 0)),
+            ]
+        ):
+            self.out.append(remote(source, target, send.at[n], recv.at[n], device))
+
+    def start(self, n):
+        self.cross[n].start()
+        self.mine[n].start()
+
+    def join(self, n):
+        self.mine[n].wait()
+        self.cross[n].wait_recv()
+        return self.own[n].astype(f32) + self.other[n].astype(f32)
+
+    def run(self):
+        for n in range(2):
+            self.own[n] = self.join(n).astype(bf16)
+            self.out[2 * n].start()
+            self.out[2 * n + 1].start()
+        half = self.half
+        for n in range(2, 6):
+            total = self.join(n)
+            side = pl.ds(0 if n % 2 == 0 else half, half)
+            self.out[n - 2].wait_recv()
+            self.own[n] = total.astype(bf16)
+            first = total[:half] if n % 2 == 0 else total[half:]
+            self.own[n, side] = (first + self.halves[n - 2].astype(f32)).astype(bf16)
+            self.out[n + 2].start()
+        total = self.join(6)
+        for n in (0, 1):
+            self.out[4 + n].wait_recv()
+            total = total + self.wholes[n].astype(f32)
+        self.own[6] = total.astype(bf16)
+        self.out[8].start()
+        total = self.join(7)
+        for n in (2, 3):
+            self.out[4 + n].wait_recv()
+            total = total + self.wholes[n].astype(f32)
+        self.out[8].wait_recv()
+        return total + self.last[...].astype(f32)
+
+    def finish(self):
+        for copy in self.out + self.cross:
+            copy.wait_send()
+
+
+def scatter_kernel(p_ref, out_ref, *scratch):
     place = my_place()
-    core = place[4]
-    sibling = sibling_of(place)
-    greet_chips(place)
-    mine, cross = [], []
+    pl.semaphore_wait(greet(chip_neighbours(place)), 4)
+    scatter = RowScatter(place, p_ref, *scratch)
     for n in range(8):
-        chip = lax.div(ctx_of(chip_peer(place, n) if n < 7 else place), 2)
-        mine.append(pltpu.make_async_copy(p_ref.at[chip, core], own.at[n], own_sem.at[n]))
-        cross.append(remote(p_ref.at[chip, 1 - core], other.at[n], send.at[n], recv.at[n], sibling))
-    for n in range(8):
-        cross[n].start()
-        mine[n].start()
-    out = []
-    for n in range(7):
-        mine[n].wait()
-        cross[n].wait_recv()
-        own[n] = (own[n].astype(f32) + other[n].astype(f32)).astype(bf16)
-        copy = remote(own.at[n], landed.at[n], csend.at[n], crecv.at[n], chip_peer(place, n))
-        copy.start()
-        out.append(copy)
-    mine[7].wait()
-    cross[7].wait_recv()
-    out_ref[...] = own[7].astype(f32) + other[7].astype(f32)
-    for n in range(7):
-        out[n].wait_recv()
-        out_ref[...] += landed[n].astype(f32)
-    for n in range(7):
-        out[n].wait_send()
-    for n in range(8):
-        cross[n].wait_send()
+        scatter.start(n)
+    out_ref[...] = scatter.run()
+    scatter.finish()
 
 
 def scatter_ctx(parts, number):
@@ -203,16 +283,7 @@
         out_shape=jax.ShapeDtypeStruct((rows, width), f32),
         in_specs=[ANY],
         out_specs=VMEM,
-        scratch_shapes=[
-            pltpu.VMEM((8, rows, width), bf16),
-            pltpu.VMEM((8, rows, width), bf16),
-            pltpu.VMEM((7, rows, width), bf16),
-            DMA((8,)),
-            DMA((8,)),
-            DMA((8,)),
-            DMA((7,)),
-            DMA((7,)),
-        ],
+        scratch_shapes=RowScatter.scratch(rows, width),
         compiler_params=pltpu.CompilerParams(
             collective_id=number, has_side_effects=True, vmem_limit_bytes=24 * 2**20
         ),
@@ -254,7 +325,7 @@
         copy.start()
     own = pltpu.make_async_copy(w_ref.at[ctx], w_out.at[dp, ctx], wlocal)
     own.start()
-    rows = RowGather(place, x_ref, x_out, *row_sems)
+    rows = RowGather(place, x_ref, lambda p: x_out.at[ctx_of(p)], x_ref.shape[0] // 2, *row_sems)
     rows.start()
     slot = lax.rem(ctx, 8)
     o_own = pltpu.make_async_copy(o_ref, o_out.at[slot], olocal)
@@ -430,6 +501,189 @@
         ),
         name="sum_grads",
     )(a, b)
+
+
+def experts_kernel(
+    ctx_ref, two_ref, cot_ref, win_ref, wdn_ref, out_ref, d_ref, gin_ref, gdn_ref,
+    two, cot, win, wdn, wide, picks, gate_slot, dg_slot, rows, tops, weighted, hidden, d_mid, d_rows,
+    gin, gdn, stage, d_stage, in_sem, out_sem, d_sem, g_sem,
+):
+    loads = [
+        pltpu.make_async_copy(two_ref, two, in_sem.at[0]),
+        pltpu.make_async_copy(cot_ref, cot, in_sem.at[1]),
+        pltpu.make_async_copy(win_ref, win, in_sem.at[2]),
+        pltpu.make_async_copy(wdn_ref, wdn, in_sem.at[3]),
+    ]
+    for load in loads:
+        load.start()
+    ctx = ctx_ref[0]
+    line = lax.broadcasted_iota(jnp.int32, (8, EXTRA), 0)
+    lane = lax.broadcasted_iota(jnp.int32, (8, EXTRA), 1)
+    start = jnp.where(line < 2, 64, jnp.where(line < 4, 0, 32))
+    chosen = jnp.logical_and(line < 6, lane == start + 2 * ctx + lax.rem(line, 2))
+    chosen = jnp.where(chosen, 1.0, 0.0).astype(bf16)
+    back = jnp.logical_and(line < 4, lane == jnp.where(line < 2, 0, 32) + 2 * ctx + lax.rem(line, 2))
+    back = jnp.where(back, 1.0, 0.0).astype(bf16)
+    before = lax.broadcasted_iota(jnp.int32, (ROWS, ROWS), 0) < lax.broadcasted_iota(
+        jnp.int32, (ROWS, ROWS), 1
+    )
+    before = jnp.where(before, 1.0, 0.0).astype(bf16)
+    slots = lax.broadcasted_iota(jnp.int32, (MOST, ROWS), 0).astype(f32)
+    loads[0].wait()
+    loads[1].wait()
+
+    def pick(c, _):
+        facts = dot_last(chosen, two[c, :, D:])
+        place = dot(facts.astype(bf16), before)
+        both = []
+        here = pl.ds(pl.multiple_of(c * MOST, MOST), MOST)
+        for e in range(2):
+            member = facts[e : e + 1]
+            onehot = jnp.where(jnp.logical_and(place[e : e + 1] == slots, member > 0.5), 1.0, 0.0)
+            gate = facts[2 + e : 3 + e] + facts[4 + e : 5 + e]
+            gate_slot[e, here] = jnp.sum(onehot * gate, axis=1, keepdims=True)
+            both.append(onehot.astype(bf16))
+        both = jnp.concatenate(both, axis=0)
+        picks[c] = both
+        taken = dot(both, two[c, :, :D]).astype(bf16)
+        rows[0, here] = taken[:MOST]
+        rows[1, here] = taken[MOST:]
+        taken = dot(both, cot[c]).astype(bf16)
+        tops[0, here] = taken[:MOST]
+        tops[1, here] = taken[MOST:]
+        return 0
+
+    lax.fori_loop(0, N_CTX, pick, 0)
+    loads[2].wait()
+    loads[3].wait()
+    for e in range(2):
+        for k in range(N_DP):
+            wide[e, :, k * ROWS : (k + 1) * ROWS] = wdn[k, e]
+    tile = 256
+    for e in range(2):
+
+        def forth(t, _):
+            here = pl.ds(pl.multiple_of(t * tile, tile), tile)
+            weight = win[:, e].reshape(D, 2 * FF)
+            down = wide[e]
+            both = dot(rows[e, here], weight)
+            gate_part, up_part = both[:, :FF], both[:, FF:]
+            sigmoid = 1.0 / (1.0 + jnp.exp(-gate_part))
+            silu = gate_part * sigmoid
+            middle = (silu * up_part).astype(bf16)
+            hidden[e, here] = middle
+            result = dot(middle, down).astype(bf16).astype(f32)
+            gate = gate_slot[e, here]
+            top = tops[e, here].astype(f32)
+            dg_slot[e, here] = jnp.sum(top * result, axis=1, keepdims=True)
+            weighted[e, here] = (result * gate).astype(bf16)
+            d_result = (top * gate).astype(bf16)
+            tops[e, here] = d_result
+            d_middle = dot_last(d_result, down)
+            d_mid[e, here, :FF] = (
+                d_middle * up_part * (sigmoid * (1.0 + gate_part * (1.0 - sigmoid)))
+            ).astype(bf16)
+            d_mid[e, here, FF:] = (d_middle * silu).astype(bf16)
+            d_rows[e, here] = dot_last(d_mid[e, here], weight).astype(bf16)
+            return 0
+
+        lax.fori_loop(0, N_CTX * MOST // tile, forth, 0)
+
+    def combine(c, _):
+        here = pl.ds(pl.multiple_of(c * MOST, MOST), MOST)
+        both = picks[c]
+        slot = lax.rem(c, 2)
+
+        @pl.when(c >= 2)
+        def _():
+            pltpu.make_async_copy(stage.at[slot], out_ref.at[c], out_sem.at[slot]).wait()
+            pltpu.make_async_copy(d_stage.at[slot], d_ref.at[c], d_sem.at[slot]).wait()
+
+        found = jnp.concatenate([d_rows[0, here], d_rows[1, here]], axis=0)
+        d_stage[slot, :, :D] = dot_first(both, found).astype(bf16)
+        lines = [
+            jnp.sum(both[e * MOST : (e + 1) * MOST].astype(f32) * dg_slot[e, here], axis=0, keepdims=True)
+            for e in range(2)
+        ]
+        high = [v.astype(bf16).astype(f32) for v in lines]
+        rest = [v - h for v, h in zip(lines, high)]
+        lines = jnp.concatenate(high + rest + [jnp.zeros((4, ROWS), f32)], axis=0).astype(bf16)
+        d_stage[slot, :, D:] = dot_first(lines, back).astype(bf16)
+        found = jnp.concatenate([weighted[0, here], weighted[1, here]], axis=0)
+        stage[slot] = dot_first(both, found).astype(bf16)
+        pltpu.make_async_copy(d_stage.at[slot], d_ref.at[c], d_sem.at[slot]).start()
+        pltpu.make_async_copy(stage.at[slot], out_ref.at[c], out_sem.at[slot]).start()
+        return 0
+
+    lax.fori_loop(0, N_CTX, combine, 0)
+    for slot in range(2):
+        pltpu.make_async_copy(stage.at[slot], out_ref.at[slot], out_sem.at[slot]).wait()
+        pltpu.make_async_copy(d_stage.at[slot], d_ref.at[slot], d_sem.at[slot]).wait()
+    for e in range(2):
+
+        def weights(k, _):
+            here = pl.ds(pl.multiple_of(k * 256, 256), 256)
+            total = dot_first(rows[e, :, here], d_mid[e]).astype(bf16)
+            gin[2 * k, e] = total[:ROWS]
+            gin[2 * k + 1, e] = total[ROWS:]
+            total = dot_first(hidden[e], tops[e, :, here]).astype(bf16)
+            gdn[2 * k, e] = total[:, :ROWS]
+            gdn[2 * k + 1, e] = total[:, ROWS:]
+            return 0
+
+        lax.fori_loop(0, D // 256, weights, 0)
+    saves = [
+        pltpu.make_async_copy(gin, gin_ref, g_sem.at[0]),
+        pltpu.make_async_copy(gdn, gdn_ref, g_sem.at[1]),
+    ]
+    for save in saves:
+        save.start()
+    for save in saves:
+        save.wait()
+
+
+def experts(ctx, two, cot, expert_in, expert_out):
+    slots = N_CTX * MOST
+    v = lambda *shape: pltpu.VMEM(shape, bf16)
+    column = pltpu.VMEM((2, slots, 1), f32)
+    return pl.pallas_call(
+        experts_kernel,
+        out_shape=(
+            jax.ShapeDtypeStruct((N_CTX, ROWS, D), bf16),
+            jax.ShapeDtypeStruct((N_CTX, ROWS, D + EXTRA), bf16),
+            jax.ShapeDtypeStruct(expert_in.shape, bf16),
+            jax.ShapeDtypeStruct(expert_out.shape, bf16),
+        ),
+        in_specs=[SMEM] + [ANY] * 4,
+        out_specs=(ANY,) * 4,
+        scratch_shapes=[
+            v(*two.shape),
+            v(*cot.shape),
+            v(*expert_in.shape),
+            v(*expert_out.shape),
+            v(2, FF, D),
+            v(N_CTX, 2 * MOST, ROWS),
+            column,
+            column,
+            v(2, slots, D),
+            v(2, slots, D),
+            v(2, slots, D),
+            v(2, slots, FF),
+            v(2, slots, 2 * FF),
+            v(2, slots, D),
+            v(*expert_in.shape),
+            v(*expert_out.shape),
+            v(2, ROWS, D),
+            v(2, ROWS, D + EXTRA),
+            DMA((4,)),
+            DMA((2,)),
+            DMA((2,)),
+            DMA((2,)),
+        ],
+        compiler_params=pltpu.CompilerParams(vmem_limit_bytes=58 * 2**20),
+        cost_estimate=pl.CostEstimate(flops=15 * 10**9, bytes_accessed=30 * 2**20, transcendentals=2**20),
+        name="experts_both_ways",
+    )(ctx, two, cot, expert_in, expert_out)
 
 
 def swap_halves(u):
@@ -626,62 +880,12 @@
     all_two = gather_ctx(sent, 2)
 
     hidden_all = all_two[:, :, :D]
-    pair = lambda at: lax.dynamic_slice_in_dim(all_two, D + at + 2 * ctx, 2, axis=2)
-    gate_all = pair(0).astype(f32) + pair(32).astype(f32)
-    member_all = pair(64)
-    triangle = jnp.tril(jnp.ones((ROWS, ROWS), bf16), -1)
-    slot = jnp.einsum("rt,cte->cer", triangle, member_all, preferred_element_type=f32)
-    turned = jnp.moveaxis(member_all, 2, 1)
-    onehot = jnp.where(
-        slot[:, :, None, :] == jnp.arange(MOST, dtype=f32)[None, None, :, None],
-        turned[:, :, None, :],
-        jnp.zeros((), bf16),
-    )
-    expert_rows = jnp.einsum("cesr,crd->ecsd", onehot, hidden_all, preferred_element_type=f32).astype(bf16)
-    expert_rows = expert_rows.reshape(2, N_CTX * MOST, D)
-    d_rows_top = jnp.einsum("cesr,crd->ecsd", onehot, cotangent_all, preferred_element_type=f32)
-    d_rows_top = d_rows_top.reshape(2, N_CTX * MOST, D)
-    gate_slot = jnp.einsum("cesr,cre->ecs", onehot.astype(f32), gate_all, precision="highest")
-    gate_slot = gate_slot.reshape(2, N_CTX * MOST, 1)
-    in_weight = jnp.moveaxis(expert_in_all, 0, 1).reshape(2, D, 2 * FF)
-    down_weight = jnp.moveaxis(expert_out_all, 0, 2).reshape(2, FF, D)
-    gate_up = jnp.einsum("esd,edf->esf", expert_rows, in_weight, preferred_element_type=f32)
-    gate_part, up_part = gate_up[..., :FF], gate_up[..., FF:]
-    expert_hidden = (jax.nn.silu(gate_part) * up_part).astype(bf16)
-    expert_result = jnp.einsum("esf,efd->esd", expert_hidden, down_weight, preferred_element_type=f32)
-    expert_result = expert_result.astype(bf16).astype(f32)
-    d_gate_slot = jnp.sum(d_rows_top * expert_result, axis=-1)
-    weighted = (expert_result * gate_slot).astype(bf16).reshape(2, N_CTX, MOST, D)
-    out_part = jnp.einsum("cesr,ecsd->crd", onehot, weighted, preferred_element_type=f32).astype(bf16)
+    out_part, d_part, grad_in, grad_down = experts(
+        ctx.reshape(1), all_two, cotangent_all, expert_in_all, expert_out_all
+    )
     output = residual + scatter_ctx(out_part, 3)
-    d_result = (d_rows_top * gate_slot).astype(bf16)
-    d_hidden = jnp.einsum("esd,efd->esf", d_result, down_weight, preferred_element_type=f32)
-    grad_down = jnp.einsum("esf,esd->efd", expert_hidden, d_result, preferred_element_type=f32)
-    sigmoid_gate = jax.nn.sigmoid(gate_part)
-    d_gate = d_hidden * up_part * (sigmoid_gate * (1.0 + gate_part * (1.0 - sigmoid_gate)))
-    d_up = d_hidden * jax.nn.silu(gate_part)
-    d_gate_up = jnp.concatenate([d_gate, d_up], axis=-1).astype(bf16)
-    grad_in = jnp.einsum("esd,esf->edf", expert_rows, d_gate_up, preferred_element_type=f32)
-    d_rows = jnp.einsum("esf,edf->esd", d_gate_up, in_weight, preferred_element_type=f32).astype(bf16)
-    d_part = jnp.einsum(
-        "cesr,ecsd->crd", onehot, d_rows.reshape(2, N_CTX, MOST, D), preferred_element_type=f32
-    ).astype(bf16)
-    d_gate_rows = jnp.sum(
-        onehot.astype(f32) * jnp.moveaxis(d_gate_slot.reshape(2, N_CTX, MOST), 0, 1)[..., None], axis=2
-    )
-    dg_high, dg_rest = halves(jnp.moveaxis(d_gate_rows, 1, 2))
-    put = lambda v: lax.dynamic_update_slice_in_dim(
-        jnp.zeros((N_CTX, ROWS, EXPERTS), bf16), v, 2 * ctx, axis=2
-    )
-    d_part = jnp.concatenate(
-        [d_part, put(dg_high), put(dg_rest), jnp.zeros((N_CTX, ROWS, EXTRA - 64), bf16)], axis=2
-    )
-    grad_in = lax.psum_scatter(
-        jnp.moveaxis(grad_in.reshape(2, N_DP, ROWS, 2 * FF), 1, 0).astype(bf16), DP, scatter_dimension=0
-    ).astype(f32)
-    grad_down = lax.psum_scatter(
-        jnp.moveaxis(grad_down.reshape(2, FF, N_DP, ROWS), 2, 0).astype(bf16), DP, scatter_dimension=0
-    ).astype(f32)
+    grad_in = lax.psum_scatter(grad_in, DP, scatter_dimension=0).astype(f32)
+    grad_down = lax.psum_scatter(grad_down, DP, scatter_dimension=0).astype(f32)
     d_sum = scatter_ctx(d_part, 4)
 
     grad_top = cotangent.astype(f32)

time: 551 us -> 437 us (0.79); the launches traced: 540 us -> 433 us
  matrix products: 60.6 us -> 20.1 us
  local copies, waits for them, and re-layouts: 72.3 us -> 32.2 us
  Pallas kernels: 332 us -> 308 us
  other arithmetic: 23.4 us -> 17.8 us
    pallas_call x0 -> x1, Pallas kernels: none -> 44.6 us  [experts(): pl.pallas_call(experts_kernel, out_shape=(jax.ShapeDtypeStruct((N_CTX, RO...]
    dot_general x12 -> x0, matrix products: 41.2 us -> none  [the longest x1 7.46 us: local(): jnp.einsum('esd,efd->esf', d_result, down_weight, preferred_element_type=...]
    pallas_call x4, Pallas kernels: 148 us -> 116 us  [scatter_ctx(): pl.pallas_call(scatter_kernel, out_shape=jax.ShapeDtypeStruct((rows, widt...]
    pallas_call x2, Pallas kernels: 85.5 us -> 63.2 us  [gather_ctx(): pl.pallas_call(gather_kernel, out_shape=jax.ShapeDtypeStruct((N_CTX,) + x...]
    pallas_call x1, Pallas kernels: 53.7 us -> 38.9 us  [entry(): pl.pallas_call(entry_kernel, out_shape=(jax.ShapeDtypeStruct((N_CTX,) + x...]
    dynamic_update_slice x2 -> x0, local copies, waits for them, and re-layouts: 10.2 us -> none  [local(): lax.dynamic_update_slice_in_dim(jnp.zeros((N_CTX, ROWS, EXPERTS), bf16),...]
    concatenate x1 -> x0, local copies, waits for them, and re-layouts: 8.43 us -> none  [local(): jnp.concatenate([d_part, put(dg_high), put(dg_rest), jnp.zeros((N_CTX, RO...]
    all_gather x2 -> x0, local copies, waits for them, and re-layouts: 7.11 us -> none  [the longest x1 4.33 us: local(): expert_out_all = lax.all_gather(expert_out, DP, axis=0)]
  transfers between devices with their start and end apart: 5 -> 5, of which waited for: 1 -> 1; matrix products, arithmetic and copies ran while one was open for 25% -> 14% of each run, Pallas kernels for 61% -> 61%
where the time goes in v2:
time: 437 us; the launch traced here: 433 us
  Pallas kernels  308 us (70%)
  waiting for transfers between devices  40.3 us (9%)
  local copies, waits for them, and re-layouts  32.2 us (7%)
  matrix products  20.1 us (5%)
  other arithmetic  17.8 us (4%)
  between operations  14.5 us (3%)
    pallas_call x4, Pallas kernels, scatter_ctx(): pl.pallas_call(scatter_kernel, out_shape=jax.ShapeDtypeStruct((rows, widt...  116 us
    pallas_call x2, Pallas kernels, gather_ctx(): pl.pallas_call(gather_kernel, out_shape=jax.ShapeDtypeStruct((N_CTX,) + x...  63.2 us
    pallas_call x1, Pallas kernels, experts(): pl.pallas_call(experts_kernel, out_shape=(jax.ShapeDtypeStruct((N_CTX, RO...  44.6 us
    pallas_call x1, Pallas kernels, entry(): pl.pallas_call(entry_kernel, out_shape=(jax.ShapeDtypeStruct((N_CTX,) + x...  38.9 us
    all_gather x1, waiting for transfers between devices, local(): cotangent_all = lax.all_gather(cotangent, CTX, axis=0)  37.7 us
    pallas_call x1, Pallas kernels, grads_out(): pl.pallas_call(grads_kernel, out_shape=(jax.ShapeDtypeStruct((N_CTX, 8, w...  23.3 us
    pallas_call x1, Pallas kernels, attend_back(): pl.pallas_call(attend_back_kernel, out_shape=jax.ShapeDtypeStruct((SEQ, 2...  13.6 us
    dot_general x3, matrix products, dot_first(): lax.dot_general(a, b, (((0,), (0,)), ((), ())), preferred_element_type=f32)  9.25 us
  transfers between devices with their start and end apart: 5, of which 1 were waited for; matrix products, arithmetic and copies ran while one was open for 14% of the time, Pallas kernels for 61%

profile of v2, /device:TPU:1, one launch (start us, length us, event | category | flops | bytes accessed | tf_op | source)
XLA Modules:
  0.0 433.4 jit_solution(8869602125459268217)
XLA Ops:
  9.4 0.7 fusion.26
  11.8 0.8 reshape.161
  12.6 0.8 reshape.159
  13.4 0.8 reshape.158
  14.2 0.7 copy.111
  15.0 0.7 copy.110
  15.8 0.8 maximum_maximum_fusion.5
  16.6 1.3 reshape.163.o_ref
  18.0 0.7 maximum_maximum_fusion.4.w_ref
  18.7 38.9 %entry_gather.1 = (bf16[16,128,1024]{2,1,0:T(8,128)(2,1)}, bf16[8,16,16,128]{3,2,1,0:T(8,128)(2,1)}, bf16[8,16,512]{2,1,0:T(8,128)(2,1)}) custom-call(bf16[128,1024]{1,0:T(8,128)(2,1)} %x_ref.1, bf16[16,16,128]{2,1,0:T(8,128)(2,1)} %maximum_maximum_fusion.4.w_ref, bf16[16,512]{1,0:T(8,128)(2,1)} %reshape.163.o_ref), custom_call_target="tpu_custom_call" | custom-call | tf_op jit(solution)/shard_map/entry_gather/pallas_call | solution.py:383
  57.6 1.1 fusion.35
  59.2 1.0 reshape.166
  60.3 3.2 multiply_reduce_fusion
  63.6 1.3 fusion.1
  64.9 2.1 copy-done.11
  67.0 2.6 fusion.21.raw_ref
  69.6 8.6 %attention_forward.1 = (bf16[2048,64]{1,0:T(8,128)(2,1)S(1)}, bf16[2048,64]{1,0:T(8,128)(2,1)S(1)}, bf16[2048,64]{1,0:T(8,128)(2,1)S(1)}, bf16[2048,64]{1,0:T(8,128)(2,1)S(1)}, f32[2048,1]{1,0:T(8,128)S(1)}) custom-call(s32[32]{0:T(128)S(1)} %select_reduce_fusion.src, s32[32]{0:T(128)S(1)} %eq.28.order, f32[2048,256]{1,0:T(8,128)} %fusion.21.raw_ref, ...), custom_call_target="tpu_custom_call" | custom-call | flops 1000000000 | bytes 6291456 | tf_op jit(solution)/shard_map/attention_forward/pallas_call | solution.py:724
  78.3 1.2 convolution_convert_fusion.1
  79.7 33.3 %scatter_rows.4 = f32[128,1024]{1,0:T(8,128)S(1)} custom-call(bf16[8,2,128,1024]{3,2,1,0:T(8,128)(2,1)S(1)} %bitcast.67), custom_call_target="tpu_custom_call" | custom-call | tf_op jit(solution)/shard_map/scatter_rows/pallas_call | solution.py:281
  114.9 0.8 concatenate.40.x_ref
  115.7 35.0 %gather_rows.2.two_ref = bf16[16,128,1152]{2,1,0:T(8,128)(2,1)} custom-call(bf16[128,1152]{1,0:T(8,128)(2,1)} %concatenate.40.x_ref), custom_call_target="tpu_custom_call" | custom-call | tf_op jit(solution)/shard_map/gather_rows/pallas_call | solution.py:168
  150.8 37.7 %all-gather.7.cloned.1.call-done = bf16[2048,1024]{1,0:T(8,128)(2,1)} async-done(((bf16[128,1024]{1,0:T(8,128)(2,1)}), bf16[2048,1024]{1,0:T(8,128)(2,1)}) %all-gather.7.cloned.1.call-update) | async-done | bytes 4194320 | tf_op jit(solution)/shard_map/all_gather | solution.py:853
  188.5 44.6 %experts_both_ways.1 = (bf16[16,128,1024]{2,1,0:T(8,128)(2,1)}, bf16[16,128,1152]{2,1,0:T(8,128)(2,1)}, bf16[8,2,128,1024]{3,2,1,0:T(8,128)(2,1)}, bf16[8,2,512,128]{3,2,1,0:T(8,128)(2,1)}) custom-call(s32[1]{0:T(128)} %bitcast.15.ctx_ref, bf16[16,128,1152]{2,1,0:T(8,128)(2,1)} %gather_rows.2.two_ref, bf16[16,128,1024]{2,1,0:T(8,128)(2,1)} %bitcast.102, ...), custom_call_target="tpu_custom_call" | custom-call | flops 15000000512 | bytes 31457280 | tf_op jit(solution)/shard_map/experts_both_ways/pallas_call | solution.py:649
  233.7 4.8 %slice.75 = bf16[16,128,1024]{2,1,0:T(8,128)(2,1)} slice(bf16[16,128,1152]{2,1,0:T(8,128)(2,1)} %gather_rows.2.two_ref), slice={[0:16], [0:128], [0:1024]} | slice | bytes 8388608 | tf_op jit(solution)/shard_map/slice | solution.py:882
  239.2 2.5 copy-done
  241.7 32.9 %scatter_rows.6 = f32[128,1152]{1,0:T(8,128)S(1)} custom-call(bf16[8,2,128,1152]{3,2,1,0:T(8,128)(2,1)S(1)} %bitcast.69), custom_call_target="tpu_custom_call" | custom-call | tf_op jit(solution)/shard_map/scatter_rows/pallas_call | solution.py:281
  276.1 0.8 concatenate.41.x_ref
  276.9 28.3 %gather_rows.3 = bf16[16,128,1152]{2,1,0:T(8,128)(2,1)} custom-call(bf16[128,1152]{1,0:T(8,128)(2,1)} %concatenate.41.x_ref), custom_call_target="tpu_custom_call" | custom-call | tf_op jit(solution)/shard_map/gather_rows/pallas_call | solution.py:168
  305.2 3.6 fusion.6
  309.1 1.0 convert_element_type.102.do_ref
  310.2 13.6 %attention_backward.1 = bf16[2048,256]{1,0:T(8,128)(2,1)} custom-call(s32[32]{0:T(128)} %copy-done.5, s32[32]{0:T(128)} %copy-done.4, bf16[2048,64]{1,0:T(8,128)(2,1)} %copy-done.7, bf16[2048,64]{1,0:T(8,128)(2,1)} %copy-done.8, bf16[2048,64]{1,0:T(8,128)(2,1)} %copy-done.9, f32[2048,1]{1,0:T(8,128)} %copy-done.6, f32[2048,64]{1,0:T(8,128)} %convert_element_type.102.do_ref, ...), custom_call_target="tpu_custom_call" | custom-call | flops 3000000000 | bytes 6291456 | tf_op jit(solution)/shard_map/attention_backward/pallas_call | solution.py:771
  323.7 2.5 convolution_convert_fusion
  326.3 23.7 %scatter_rows.7 = f32[128,1024]{1,0:T(8,128)S(1)} custom-call(bf16[8,2,128,1024]{3,2,1,0:T(8,128)(2,1)S(1)} %bitcast.68), custom_call_target="tpu_custom_call" | custom-call | tf_op jit(solution)/shard_map/scatter_rows/pallas_call | solution.py:281
  350.0 0.9 copy.121
  351.2 0.9 copy.120
  352.1 3.8 fusion.37
  355.9 0.8 slice.128
  356.7 1.2 copy.119
  357.9 1.7 fusion.18
  359.6 3.8 fusion.2
  363.3 1.0 concatenate.46
  364.4 1.3 maximum_maximum_fusion.1.a_ref
  365.7 23.3 %sum_grads.1 = (f32[16,8,256]{2,1,0:T(8,128)S(1)}, f32[8,8,1152]{2,1,0:T(8,128)S(1)}) custom-call(bf16[8,128,256]{2,1,0:T(8,128)(2,1)S(1)} %maximum_maximum_fusion.1.a_ref, f32[8,8,1152]{2,1,0:T(8,128)S(1)} %bitcast.71), custom_call_target="tpu_custom_call" | custom-call | tf_op jit(solution)/shard_map/sum_grads/pallas_call | solution.py:489
  390.3 2.2 copy-done.1
  392.5 26.1 %scatter_rows.5 = f32[128,1024]{1,0:T(8,128)S(1)} custom-call(bf16[8,2,128,1024]{3,2,1,0:T(8,128)(2,1)S(1)} %bitcast.70), custom_call_target="tpu_custom_call" | custom-call | tf_op jit(solution)/shard_map/scatter_rows/pallas_call | solution.py:281
  421.6 1.2 fusion.15
  422.8 1.8 bitcast_convert_fusion.1
  424.6 2.1 bitcast_convert_fusion
  (107 shorter events, 14.3 us)
Async XLA Ops:
  7.2 143.6 %all-gather.11.cloned.1.call-start = ((), (), s32[]{:S(2)}) async-start(), calls=%async_computation.6 | async-start | bytes 2359296 | tf_op jit(solution)/shard_map/all_gather | solution.py:852
  7.9 142.9 %all-gather.9.cloned.1.call-start = ((), (), s32[]{:S(2)}) async-start(), calls=%async_computation.5 | async-start | bytes 4718592 | tf_op jit(solution)/shard_map/all_gather | solution.py:851
  8.7 179.8 %all-gather.7.cloned.1.call-start = ((), (), s32[]{:S(2)}) async-start(), calls=%async_computation.4 | async-start | bytes 4456448 | tf_op jit(solution)/shard_map/all_gather | solution.py:853
  9.4 413.4 %reduce-scatter.5.cloned.1.call-start = ((), (), s32[]{:S(2)}) async-start(), calls=%async_computation.3 | async-start | bytes 2359296 | tf_op jit(solution)/shard_map/reduce_scatter | solution.py:888
  11.8 57.8 %copy-start.4 = (s32[32]{0:T(128)}, s32[32]{0:T(128)S(1)}, u32[]{:S(2)}) copy-start(s32[32]{0:T(128)S(1)} %eq.28.order) | copy-start | bytes 388
  59.2 5.7 %copy-start.17 = (bf16[256]{0:T(256)(128)(2,1)}, bf16[256]{0:T(256)(128)(2,1)S(1)}, u32[]{:S(2)}) copy-start(bf16[256]{0:T(256)(128)(2,1)S(1)} %pad.6.clone) | copy-start | bytes 1540
  60.1 3.5 copy-start.10
  60.3 9.4 %copy-start.5 = (s32[32]{0:T(128)}, s32[32]{0:T(128)S(1)}, u32[]{:S(2)}) copy-start(s32[32]{0:T(128)S(1)} %select_reduce_fusion.src) | copy-start | bytes 388
  64.9 2.1 copy-start.11
  64.9 4.7 %copy-start.2 = (f32[2048,128]{1,0:T(8,128)S(1)}, f32[2048,128]{1,0:T(8,128)}, u32[]{:S(2)}) copy-start(f32[2048,128]{1,0:T(8,128)} %constant.54.clone.cos_ref) | copy-start | bytes 3145732
  64.9 4.7 %copy-start.3 = (f32[2048,128]{1,0:T(8,128)S(1)}, f32[2048,128]{1,0:T(8,128)}, u32[]{:S(2)}) copy-start(f32[2048,128]{1,0:T(8,128)} %constant.55.clone.sin_ref) | copy-start | bytes 3145732
  78.2 1.3 copy-start.6
  78.2 1.3 copy-start.7
  78.3 1.3 copy-start.8
  78.3 1.4 copy-start.9
  79.7 33.6 %copy-start.12 = (bf16[128,1024]{1,0:T(8,128)(2,1)S(1)}, bf16[128,1024]{1,0:T(8,128)(2,1)}, u32[]{:S(2)}) copy-start(bf16[128,1024]{1,0:T(8,128)(2,1)} %x_ref.1) | copy-start | bytes 786436
  233.1 191.4 %reduce-scatter.3.cloned.1.call-start = ((), (), s32[]{:S(2)}) async-start(), calls=%async_computation.2 | async-start | bytes 4718592 | tf_op jit(solution)/shard_map/reduce_scatter | solution.py:887
  233.7 42.2 %copy-start.13 = (bf16[128,1024]{1,0:T(8,128)(2,1)S(1)}, bf16[128,1024]{1,0:T(8,128)(2,1)}, u32[]{:S(2)}) copy-start(bf16[128,1024]{1,0:T(8,128)(2,1)} %param.16) | copy-start | bytes 786436
  239.2 2.5 copy-start
  275.3 0.6 copy-start.15
  310.2 13.6 %copy-start.18 = (bf16[256]{0:T(256)(128)(2,1)S(1)}, bf16[256]{0:T(256)(128)(2,1)}, u32[]{:S(2)}) copy-start(bf16[256]{0:T(256)(128)(2,1)} %copy-done.17) | copy-start | bytes 1540
  326.3 24.7 %copy-start.14 = (f32[128]{0:T(128)S(1)}, f32[128]{0:T(128)}, u32[]{:S(2)}) copy-start(f32[128]{0:T(128)} %get-tuple-element.61) | copy-start | bytes 1540
  355.9 8.5 %copy-start.19 = (bf16[256]{0:T(256)(128)(2,1)S(1)}, bf16[256]{0:T(256)(128)(2,1)}, u32[]{:S(2)}) copy-start(bf16[256]{0:T(256)(128)(2,1)} %pad.3.clone) | copy-start | bytes 1540
  364.4 57.2 %copy-start.16 = (f32[128]{0:T(128)S(1)}, f32[128]{0:T(128)}, u32[]{:S(2)}) copy-start(f32[128]{0:T(128)} %copy-done.15) | copy-start | bytes 1540
  390.3 2.2 copy-start.1
Sparse Core Ops, SparseCore 0:
  9.7 54.1 all-gather.10
  65.5 60.5 all-gather.8
  128.5 59.9 all-gather.6
  233.3 39.0 reduce-scatter.4
  274.6 57.7 reduce-scatter.2

commit v3 on v2

--- a/solution.py
+++ b/solution.py
@@ -195,7 +195,7 @@
             DMA((9,)),
         ]
 
-    def __init__(self, place, p_ref, own, other, halves, wholes, last, own_sem, fsend, frecv, send, recv):
+    def __init__(self, place, part, own, other, halves, wholes, last, own_sem, fsend, frecv, send, recv):
         self.own, self.other, self.halves, self.wholes, self.last = own, other, halves, wholes, last
         core = place[4]
         half = own.shape[1] // 2
@@ -203,9 +203,9 @@
         self.mine, self.cross = [], []
         for n, (dy, dx) in enumerate(SPREAD):
             chip = lax.div(ctx_of(beside(place, dy, dx)), 2)
-            self.mine.append(pltpu.make_async_copy(p_ref.at[chip, core], own.at[n], own_sem.at[n]))
+            self.mine.append(pltpu.make_async_copy(part(chip, core), own.at[n], own_sem.at[n]))
             self.cross.append(
-                remote(p_ref.at[chip, 1 - core], other.at[n], fsend.at[n], frecv.at[n], sibling_of(place))
+                remote(part(chip, 1 - core), other.at[n], fsend.at[n], frecv.at[n], sibling_of(place))
             )
         right, left = beside(place, 0, 1), beside(place, 0, 3)
         self.out = []
@@ -233,32 +233,34 @@
         self.cross[n].wait_recv()
         return self.own[n].astype(f32) + self.other[n].astype(f32)
 
-    def run(self):
-        for n in range(2):
+    def step(self, n):
+        if n < 2:
             self.own[n] = self.join(n).astype(bf16)
             self.out[2 * n].start()
             self.out[2 * n + 1].start()
-        half = self.half
-        for n in range(2, 6):
+        elif n < 6:
             total = self.join(n)
+            half = self.half
             side = pl.ds(0 if n % 2 == 0 else half, half)
             self.out[n - 2].wait_recv()
             self.own[n] = total.astype(bf16)
             first = total[:half] if n % 2 == 0 else total[half:]
             self.own[n, side] = (first + self.halves[n - 2].astype(f32)).astype(bf16)
             self.out[n + 2].start()
-        total = self.join(6)
-        for n in (0, 1):
-            self.out[4 + n].wait_recv()
-            total = total + self.wholes[n].astype(f32)
-        self.own[6] = total.astype(bf16)
-        self.out[8].start()
-        total = self.join(7)
-        for n in (2, 3):
-            self.out[4 + n].wait_recv()
-            total = total + self.wholes[n].astype(f32)
-        self.out[8].wait_recv()
-        return total + self.last[...].astype(f32)
+        elif n == 6:
+            total = self.join(6)
+            for m in (0, 1):
+                self.out[4 + m].wait_recv()
+                total = total + self.wholes[m].astype(f32)
+            self.own[6] = total.astype(bf16)
+            self.out[8].start()
+        else:
+            total = self.join(7)
+            for m in (2, 3):
+                self.out[4 + m].wait_recv()
+                total = total + self.wholes[m].astype(f32)
+            self.out[8].wait_recv()
+            return total + self.last[...].astype(f32)
 
     def finish(self):
         for copy in self.out + self.cross:
@@ -268,10 +270,12 @@
 def scatter_kernel(p_ref, out_ref, *scratch):
     place = my_place()
     pl.semaphore_wait(greet(chip_neighbours(place)), 4)
-    scatter = RowScatter(place, p_ref, *scratch)
+    scatter = RowScatter(place, lambda chip, core: p_ref.at[chip, core], *scratch)
     for n in range(8):
         scatter.start(n)
-    out_ref[...] = scatter.run()
+    for n in range(7):
+        scatter.step(n)
+    out_ref[...] = scatter.step(7)
     scatter.finish()
 
 
@@ -291,8 +295,8 @@
     )(parts)
 
 
-def entry_kernel(x_ref, w_ref, o_ref, x_out, w_out, o_out, *sems):
-    row_sems, rest = sems[:5], sems[5:]
+def entry_kernel(x_ref, w_ref, o_ref, m_ref, x_out, w_out, o_out, o_mid, *sems):
+    row_sems, o_sems, rest = sems[:5], sems[5:10], sems[10:]
     wlocal, wsend, wrecv, psend, precv, olocal, osend, orecv = rest
     place = my_place()
     dp, ctx = dp_of(place), ctx_of(place)
@@ -300,100 +304,70 @@
         [device_at(dp, lax.rem(ctx + k, N_CTX)) for k in range(1, N_CTX)]
         + [device_at(lax.rem(dp + k, N_DP), ctx) for k in range(1, N_DP)]
     )
-    o_ctx = 2 * dp + lax.div(ctx, 8)
-    o_home = lax.div(ctx, 2)
-    from_ctx = 8 * lax.rem(ctx, 2)
-    o_self = o_ctx == ctx
-    for t in range(8):
-        here = jnp.logical_and(o_home == dp, from_ctx + t == ctx)
-
-        @pl.when(jnp.logical_not(here))
-        def _():
-            pl.semaphore_signal(
-                barrier, inc=1, device_id=device_at(o_home, from_ctx + t), device_id_type=MESH_ID
-            )
-
-    pl.semaphore_wait(barrier, 30 - jnp.where(o_self, 1, 0))
-
-    first = []
+    pl.semaphore_wait(barrier, 22)
+
+    def o_place(k):
+        return o_mid.at[pl.ds(pl.multiple_of(k * 16, 16), 16)]
+
+    first, second, third = [], [], []
+    for k in range(1, N_DP):
+        to = lax.rem(dp + k, N_DP)
+        third.append(remote(o_ref, o_place(dp), osend.at[k], orecv.at[k], device_at(to, ctx)))
+        second.append(remote(w_out.at[dp], w_out.at[dp], psend.at[k], precv.at[k], device_at(to, ctx)))
     for k in range(1, N_CTX):
         to = lax.rem(ctx + k, N_CTX)
         first.append(
             remote(w_ref.at[to], w_out.at[dp, ctx], wsend.at[k], wrecv.at[k], device_at(dp, to))
         )
-    for copy in first:
+    for copy in third + first:
         copy.start()
-    own = pltpu.make_async_copy(w_ref.at[ctx], w_out.at[dp, ctx], wlocal)
-    own.start()
+    owns = [
+        pltpu.make_async_copy(w_ref.at[ctx], w_out.at[dp, ctx], wlocal),
+        pltpu.make_async_copy(o_ref, o_place(dp), olocal.at[0]),
+        pltpu.make_async_copy(m_ref, o_mid.at[pl.ds(128, 32)], olocal.at[1]),
+    ]
+    for copy in owns:
+        copy.start()
     rows = RowGather(place, x_ref, lambda p: x_out.at[ctx_of(p)], x_ref.shape[0] // 2, *row_sems)
     rows.start()
-    slot = lax.rem(ctx, 8)
-    o_own = pltpu.make_async_copy(o_ref, o_out.at[slot], olocal)
-
-    def o_copy(k):
-        return remote(o_ref, o_out.at[slot], osend.at[k], orecv.at[slot], device_at(k, o_ctx))
-
-    for k in range(8):
-        here = jnp.logical_and(o_self, dp == k)
-
-        @pl.when(here)
-        def _():
-            o_own.start()
-
-        @pl.when(jnp.logical_not(here))
-        def _():
-            o_copy(k).start()
-
-    own.wait()
+    for copy in owns:
+        copy.wait()
+    for copy in third:
+        copy.wait_recv()
+    outs = RowGather(place, o_mid, lambda p: o_out.at[ctx_of(p)], 80, *o_sems)
+    outs.start()
     for copy in first:
         copy.wait_recv()
-    second = []
-    for k in range(1, N_DP):
-        to = lax.rem(dp + k, N_DP)
-        second.append(remote(w_out.at[dp], w_out.at[dp], psend.at[k], precv.at[k], device_at(to, ctx)))
     for copy in second:
         copy.start()
-    rows.pass_on()
+    for n in range(9):
+        rows.step(n)
+        outs.step(n)
     rows.finish()
+    outs.finish()
     for copy in second:
         copy.wait_recv()
-    for t in range(8):
-        here = jnp.logical_and(o_home == dp, from_ctx + t == ctx)
-
-        @pl.when(jnp.logical_not(here))
-        def _():
-            remote(o_ref, o_out.at[t], osend.at[0], orecv.at[t], device_at(dp, ctx)).wait_recv()
-
-    for k in range(8):
-        here = jnp.logical_and(o_self, dp == k)
-
-        @pl.when(here)
-        def _():
-            o_own.wait()
-
-        @pl.when(jnp.logical_not(here))
-        def _():
-            o_copy(k).wait_send()
-
-    for copy in first + second:
+    for copy in first + second + third:
         copy.wait_send()
 
 
-def entry(x, w, o, number):
+def entry(x, w, o, m, number):
     return pl.pallas_call(
         entry_kernel,
         out_shape=(
             jax.ShapeDtypeStruct((N_CTX,) + x.shape, x.dtype),
             jax.ShapeDtypeStruct((N_DP,) + w.shape, w.dtype),
-            jax.ShapeDtypeStruct((8,) + o.shape, o.dtype),
+            jax.ShapeDtypeStruct((N_CTX, 160, 512), bf16),
         ),
-        in_specs=[ANY] * 3,
+        in_specs=[ANY] * 4,
         out_specs=(ANY, ANY, ANY),
-        scratch_shapes=RowGather.scratch
-        + [DMA, DMA((16,)), DMA((16,)), DMA((8,)), DMA((8,)), DMA, DMA((8,)), DMA((8,))],
+        scratch_shapes=[pltpu.VMEM((160, 512), bf16)]
+        + RowGather.scratch
+        + RowGather.scratch
+        + [DMA, DMA((16,)), DMA((16,)), DMA((8,)), DMA((8,)), DMA((2,)), DMA((8,)), DMA((8,))],
         compiler_params=pltpu.CompilerParams(collective_id=number, has_side_effects=True),
         name="entry_gather",
-    )(x, w, o)
+    )(x, w, o, m)
 
 
 def grads_kernel(
@@ -504,19 +478,24 @@
 
 
 def experts_kernel(
-    ctx_ref, two_ref, cot_ref, win_ref, wdn_ref, out_ref, d_ref, gin_ref, gdn_ref,
-    two, cot, win, wdn, wide, picks, gate_slot, dg_slot, rows, tops, weighted, hidden, d_mid, d_rows,
-    gin, gdn, stage, d_stage, in_sem, out_sem, d_sem, g_sem,
+    hid_ref, facts_ref, cot_ref, w_ref, out_ref, d_ref, g_ref, out_parts, d_parts,
+    pool, facts_all, win, wide, picks, gate_slot, dg_slot, rows, tops, result, hidden, d_mid,
+    stage, d_stage, in_sem, out_sem, d_sem, g_sem, *scatters,
 ):
     loads = [
-        pltpu.make_async_copy(two_ref, two, in_sem.at[0]),
-        pltpu.make_async_copy(cot_ref, cot, in_sem.at[1]),
-        pltpu.make_async_copy(win_ref, win, in_sem.at[2]),
-        pltpu.make_async_copy(wdn_ref, wdn, in_sem.at[3]),
+        pltpu.make_async_copy(facts_ref, facts_all, in_sem.at[0]),
+        pltpu.make_async_copy(hid_ref, pool.at[:, :, 0], in_sem.at[1]),
+        pltpu.make_async_copy(w_ref, win, in_sem.at[2]),
     ]
     for load in loads:
         load.start()
-    ctx = ctx_ref[0]
+    place = my_place()
+    ctx = ctx_of(place)
+    pl.semaphore_wait(greet(chip_neighbours(place)), 4)
+    gather = RowGather(
+        place, cot_ref, lambda p: pool.at[p[2] * 4 + p[3], p[4], 1], ROWS // 2, *scatters[20:]
+    )
+    gather.start()
     line = lax.broadcasted_iota(jnp.int32, (8, EXTRA), 0)
     lane = lax.broadcasted_iota(jnp.int32, (8, EXTRA), 1)
     start = jnp.where(line < 2, 64, jnp.where(line < 4, 0, 32))
@@ -529,138 +508,182 @@
     )
     before = jnp.where(before, 1.0, 0.0).astype(bf16)
     slots = lax.broadcasted_iota(jnp.int32, (MOST, ROWS), 0).astype(f32)
-    loads[0].wait()
-    loads[1].wait()
+    for load in loads[:2]:
+        load.wait()
 
     def pick(c, _):
-        facts = dot_last(chosen, two[c, :, D:])
-        place = dot(facts.astype(bf16), before)
+        facts = dot_last(chosen, facts_all[c])
+        order = dot(facts.astype(bf16), before)
         both = []
         here = pl.ds(pl.multiple_of(c * MOST, MOST), MOST)
         for e in range(2):
             member = facts[e : e + 1]
-            onehot = jnp.where(jnp.logical_and(place[e : e + 1] == slots, member > 0.5), 1.0, 0.0)
+            onehot = jnp.where(jnp.logical_and(order[e : e + 1] == slots, member > 0.5), 1.0, 0.0)
             gate = facts[2 + e : 3 + e] + facts[4 + e : 5 + e]
             gate_slot[e, here] = jnp.sum(onehot * gate, axis=1, keepdims=True)
             both.append(onehot.astype(bf16))
         both = jnp.concatenate(both, axis=0)
         picks[c] = both
-        taken = dot(both, two[c, :, :D]).astype(bf16)
+        taken = dot(both, pool[lax.div(c, 2), lax.rem(c, 2), 0]).astype(bf16)
         rows[0, here] = taken[:MOST]
         rows[1, here] = taken[MOST:]
-        taken = dot(both, cot[c]).astype(bf16)
+        return 0
+
+    lax.fori_loop(0, N_CTX, pick, 0)
+    for n in range(3):
+        gather.step(n)
+    loads[2].wait()
+    for e in range(2):
+        for k in range(N_DP):
+            for q in range(8):
+                wide[e, q * 64 : (q + 1) * 64, k * ROWS : (k + 1) * ROWS] = win[
+                    k, e, ROWS:, q * ROWS : (q + 1) * ROWS
+                ]
+    tile = 256
+
+    def pick_tops(c, _):
+        here = pl.ds(pl.multiple_of(c * MOST, MOST), MOST)
+        taken = dot(picks[c], pool[lax.div(c, 2), lax.rem(c, 2), 1]).astype(bf16)
         tops[0, here] = taken[:MOST]
         tops[1, here] = taken[MOST:]
         return 0
 
-    lax.fori_loop(0, N_CTX, pick, 0)
-    loads[2].wait()
-    loads[3].wait()
-    for e in range(2):
-        for k in range(N_DP):
-            wide[e, :, k * ROWS : (k + 1) * ROWS] = wdn[k, e]
-    tile = 256
-    for e in range(2):
-
-        def forth(t, _):
-            here = pl.ds(pl.multiple_of(t * tile, tile), tile)
-            weight = win[:, e].reshape(D, 2 * FF)
-            down = wide[e]
-            both = dot(rows[e, here], weight)
-            gate_part, up_part = both[:, :FF], both[:, FF:]
-            sigmoid = 1.0 / (1.0 + jnp.exp(-gate_part))
-            silu = gate_part * sigmoid
-            middle = (silu * up_part).astype(bf16)
-            hidden[e, here] = middle
-            result = dot(middle, down).astype(bf16).astype(f32)
-            gate = gate_slot[e, here]
-            top = tops[e, here].astype(f32)
-            dg_slot[e, here] = jnp.sum(top * result, axis=1, keepdims=True)
-            weighted[e, here] = (result * gate).astype(bf16)
-            d_result = (top * gate).astype(bf16)
-            tops[e, here] = d_result
-            d_middle = dot_last(d_result, down)
-            d_mid[e, here, :FF] = (
-                d_middle * up_part * (sigmoid * (1.0 + gate_part * (1.0 - sigmoid)))
-            ).astype(bf16)
-            d_mid[e, here, FF:] = (d_middle * silu).astype(bf16)
-            d_rows[e, here] = dot_last(d_mid[e, here], weight).astype(bf16)
-            return 0
-
-        lax.fori_loop(0, N_CTX * MOST // tile, forth, 0)
-
-    def combine(c, _):
+    def forth(e, t):
+        here = pl.ds(t * tile, tile)
+        both = dot(rows[e, here], win[:, e, :ROWS].reshape(D, 2 * FF))
+        gate_part, up_part = both[:, :FF], both[:, FF:]
+        sigmoid = 1.0 / (1.0 + jnp.exp(-gate_part))
+        silu = gate_part * sigmoid
+        middle = (silu * up_part).astype(bf16)
+        hidden[e, here] = middle
+        d_mid[e, here, :FF] = (up_part * (sigmoid * (1.0 + gate_part * (1.0 - sigmoid)))).astype(bf16)
+        d_mid[e, here, FF:] = silu.astype(bf16)
+        result[e, here] = dot(middle, wide[e]).astype(bf16)
+
+    def backward(e, t):
+        here = pl.ds(t * tile, tile)
+        top = tops[e, here].astype(f32)
+        dg_slot[e, here] = jnp.sum(top * result[e, here].astype(f32), axis=1, keepdims=True)
+        d_result = (top * gate_slot[e, here]).astype(bf16)
+        tops[e, here] = d_result
+        d_middle = dot_last(d_result, wide[e])
+        d_mid[e, here, :FF] = (d_middle * d_mid[e, here, :FF].astype(f32)).astype(bf16)
+        d_mid[e, here, FF:] = (d_middle * d_mid[e, here, FF:].astype(f32)).astype(bf16)
+        weight = win[:, e, :ROWS].reshape(D, 2 * FF)
+        result[e, here] = dot_last(d_mid[e, here], weight).astype(bf16)
+
+    def combined(c, width, staged, out, sem, with_gates):
         here = pl.ds(pl.multiple_of(c * MOST, MOST), MOST)
         both = picks[c]
         slot = lax.rem(c, 2)
 
         @pl.when(c >= 2)
         def _():
-            pltpu.make_async_copy(stage.at[slot], out_ref.at[c], out_sem.at[slot]).wait()
-            pltpu.make_async_copy(d_stage.at[slot], d_ref.at[c], d_sem.at[slot]).wait()
-
-        found = jnp.concatenate([d_rows[0, here], d_rows[1, here]], axis=0)
-        d_stage[slot, :, :D] = dot_first(both, found).astype(bf16)
-        lines = [
-            jnp.sum(both[e * MOST : (e + 1) * MOST].astype(f32) * dg_slot[e, here], axis=0, keepdims=True)
-            for e in range(2)
-        ]
-        high = [v.astype(bf16).astype(f32) for v in lines]
-        rest = [v - h for v, h in zip(lines, high)]
-        lines = jnp.concatenate(high + rest + [jnp.zeros((4, ROWS), f32)], axis=0).astype(bf16)
-        d_stage[slot, :, D:] = dot_first(lines, back).astype(bf16)
-        found = jnp.concatenate([weighted[0, here], weighted[1, here]], axis=0)
-        stage[slot] = dot_first(both, found).astype(bf16)
-        pltpu.make_async_copy(d_stage.at[slot], d_ref.at[c], d_sem.at[slot]).start()
-        pltpu.make_async_copy(stage.at[slot], out_ref.at[c], out_sem.at[slot]).start()
-        return 0
-
-    lax.fori_loop(0, N_CTX, combine, 0)
-    for slot in range(2):
-        pltpu.make_async_copy(stage.at[slot], out_ref.at[slot], out_sem.at[slot]).wait()
-        pltpu.make_async_copy(d_stage.at[slot], d_ref.at[slot], d_sem.at[slot]).wait()
+            pltpu.make_async_copy(staged.at[slot], out.at[c], sem.at[slot]).wait()
+
+        found = [result[0, here], result[1, here]]
+        if not with_gates:
+            found = [(found[e].astype(f32) * gate_slot[e, here]).astype(bf16) for e in range(2)]
+        found = jnp.concatenate(found, axis=0)
+        staged[slot, :, :D] = dot_first(both, found).astype(bf16)
+        if with_gates:
+            lines = [
+                jnp.sum(
+                    both[e * MOST : (e + 1) * MOST].astype(f32) * dg_slot[e, here], axis=0, keepdims=True
+                )
+                for e in range(2)
+            ]
+            high = [v.astype(bf16).astype(f32) for v in lines]
+            rest = [v - h for v, h in zip(lines, high)]
+            lines = jnp.concatenate(high + rest + [jnp.zeros((4, ROWS), f32)], axis=0).astype(bf16)
+            staged[slot, :, D:] = dot_first(lines, back).astype(bf16)
+        pltpu.make_async_copy(staged.at[slot], out.at[c], sem.at[slot]).start()
+
+    def combine(staged, out, sem, with_gates):
+        def one(c, _):
+            combined(c, D, staged, out, sem, with_gates)
+            return 0
+
+        lax.fori_loop(0, N_CTX, one, 0)
+        for slot in range(2):
+            pltpu.make_async_copy(staged.at[slot], out.at[slot], sem.at[slot]).wait()
+
+    def chips(ref):
+        return lambda chip, core: ref.at[chip * 2 + core]
+
     for e in range(2):
-
-        def weights(k, _):
-            here = pl.ds(pl.multiple_of(k * 256, 256), 256)
-            total = dot_first(rows[e, :, here], d_mid[e]).astype(bf16)
-            gin[2 * k, e] = total[:ROWS]
-            gin[2 * k + 1, e] = total[ROWS:]
-            total = dot_first(hidden[e], tops[e, :, here]).astype(bf16)
-            gdn[2 * k, e] = total[:, :ROWS]
-            gdn[2 * k + 1, e] = total[:, ROWS:]
-            return 0
-
-        lax.fori_loop(0, D // 256, weights, 0)
+        for t in range(3):
+            forth(e, t)
+            gather.step(3 + 3 * e + t)
+    combine(stage, out_parts, out_sem, False)
+    first = RowScatter(place, chips(out_parts), *scatters[:10])
+    second = RowScatter(place, chips(d_parts), *scatters[10:20])
+    for n in range(8):
+        first.start(n)
+    gather.finish()
+    lax.fori_loop(0, N_CTX, pick_tops, 0)
+    plan = [(), (0, 1), (), (2, 3), (), (4, 5)]
+    for e in range(2):
+        for t in range(3):
+            backward(e, t)
+            for n in plan[3 * e + t]:
+                first.step(n)
+    combine(d_stage, d_parts, d_sem, True)
+    for n in range(8):
+        second.start(n)
+    first.step(6)
+    out_ref[...] = first.step(7)
+
+    def weights(e, k):
+        here = pl.ds(k * 256, 256)
+        total = dot_first(rows[e, :, here], d_mid[e]).astype(bf16)
+        pool[2 * k, e, 0] = total[:ROWS]
+        pool[2 * k + 1, e, 0] = total[ROWS:]
+        total = dot_first(hidden[e], tops[e, :, here]).astype(bf16)
+        for q in range(8):
+            pool[2 * k, e, 1, :64, q * ROWS : (q + 1) * ROWS] = total[q * 64 : (q + 1) * 64, :ROWS]
+            pool[2 * k + 1, e, 1, :64, q * ROWS : (q + 1) * ROWS] = total[q * 64 : (q + 1) * 64, ROWS:]
+
+    plan = [(), (0, 1), (), (2, 3), (), (4, 5), (), ()]
+    for e in range(2):
+        for k in range(4):
+            weights(e, k)
+            for n in plan[4 * e + k]:
+                second.step(n)
     saves = [
-        pltpu.make_async_copy(gin, gin_ref, g_sem.at[0]),
-        pltpu.make_async_copy(gdn, gdn_ref, g_sem.at[1]),
+        pltpu.make_async_copy(pool.at[:, :, 0], g_ref.at[:, :, :ROWS], g_sem.at[0]),
+        pltpu.make_async_copy(pool.at[:, :, 1, :64], g_ref.at[:, :, ROWS:], g_sem.at[1]),
     ]
     for save in saves:
         save.start()
+    second.step(6)
+    d_ref[...] = second.step(7)
     for save in saves:
         save.wait()
-
-
-def experts(ctx, two, cot, expert_in, expert_out):
+    first.finish()
+    second.finish()
+
+
+def experts(hid, facts, cot, weights, number):
     slots = N_CTX * MOST
     v = lambda *shape: pltpu.VMEM(shape, bf16)
     column = pltpu.VMEM((2, slots, 1), f32)
+    blocks = (8, 2, ROWS, D)
     return pl.pallas_call(
         experts_kernel,
         out_shape=(
+            jax.ShapeDtypeStruct((ROWS, D), f32),
+            jax.ShapeDtypeStruct((ROWS, D + EXTRA), f32),
+            jax.ShapeDtypeStruct(weights.shape, bf16),
             jax.ShapeDtypeStruct((N_CTX, ROWS, D), bf16),
             jax.ShapeDtypeStruct((N_CTX, ROWS, D + EXTRA), bf16),
-            jax.ShapeDtypeStruct(expert_in.shape, bf16),
-            jax.ShapeDtypeStruct(expert_out.shape, bf16),
         ),
-        in_specs=[SMEM] + [ANY] * 4,
-        out_specs=(ANY,) * 4,
+        in_specs=[ANY] * 4,
+        out_specs=(VMEM, VMEM, ANY, ANY, ANY),
         scratch_shapes=[
-            v(*two.shape),
-            v(*cot.shape),
-            v(*expert_in.shape),
-            v(*expert_out.shape),
+            v(8, 2, 2, ROWS, D),
+            v(N_CTX, ROWS, EXTRA),
+            v(*weights.shape),
             v(2, FF, D),
             v(N_CTX, 2 * MOST, ROWS),
             column,
@@ -670,20 +693,22 @@
             v(2, slots, D),
             v(2, slots, FF),
             v(2, slots, 2 * FF),
-            v(2, slots, D),
-            v(*expert_in.shape),
-            v(*expert_out.shape),
             v(2, ROWS, D),
             v(2, ROWS, D + EXTRA),
-            DMA((4,)),
+            DMA((3,)),
             DMA((2,)),
             DMA((2,)),
             DMA((2,)),
-        ],
-        compiler_params=pltpu.CompilerParams(vmem_limit_bytes=58 * 2**20),
+        ]
+        + RowScatter.scratch(ROWS, D)
+        + RowScatter.scratch(ROWS, D + EXTRA)
+        + RowGather.scratch,
+        compiler_params=pltpu.CompilerParams(
+            collective_id=number, has_side_effects=True, vmem_limit_bytes=61 * 2**20
+        ),
         cost_estimate=pl.CostEstimate(flops=15 * 10**9, bytes_accessed=30 * 2**20, transcendentals=2**20),
         name="experts_both_ways",
-    )(ctx, two, cot, expert_in, expert_out)
+    )(hid.reshape(blocks), facts, cot, weights)
 
 
 def swap_halves(u):
@@ -691,7 +716,10 @@
     return jnp.where(lax.rem(lane, 64) < 32, pltpu.roll(u, 96, 1), pltpu.roll(u, 32, 1))
 
 
-def attend_kernel(src, order, raw_ref, cos_ref, sin_ref, o_ref, q_ref, k_ref, v_ref, lse_ref, out_nat):
+def attend_kernel(
+    src, order, raw_ref, cos_ref, sin_ref, o_ref, padded, q_ref, k_ref, v_ref, lse_ref, out_nat
+):
+    core = lax.axis_index("core")
     for b in range(SEQ // BLOCK):
         rows = pl.ds(pl.multiple_of(src[b] * BLOCK, BLOCK), BLOCK)
         here = pl.ds(b * BLOCK, BLOCK)
@@ -716,21 +744,75 @@
         out_nat[here, :] = dot(probs, v_ref[0:length, :])
     for b in range(SEQ // BLOCK):
         rows = pl.ds(pl.multiple_of(order[b] * BLOCK, BLOCK), BLOCK)
-        o_ref[pl.ds(b * BLOCK, BLOCK), :] = out_nat[rows, :].astype(bf16)
+        here = pl.ds(b * BLOCK, BLOCK)
+        out = out_nat[rows, :].astype(bf16)
+        o_ref[here, :] = out
+        empty = jnp.zeros_like(out)
+        padded[here, :] = jnp.where(
+            core == 0, jnp.concatenate([out, empty], axis=1), jnp.concatenate([empty, out], axis=1)
+        )
 
 
 def attend(src, order, raw, cosine, sine):
     head = jax.ShapeDtypeStruct((SEQ, HEAD_DIM), bf16)
     return pl.pallas_call(
         attend_kernel,
-        out_shape=(head, head, head, head, jax.ShapeDtypeStruct((SEQ, 1), f32)),
+        out_shape=(
+            head,
+            jax.ShapeDtypeStruct((SEQ, 128), bf16),
+            head,
+            head,
+            head,
+            jax.ShapeDtypeStruct((SEQ, 1), f32),
+        ),
         in_specs=[SMEM, SMEM, VMEM, VMEM, VMEM],
-        out_specs=(VMEM,) * 5,
+        out_specs=(VMEM,) * 6,
         scratch_shapes=[pltpu.VMEM((SEQ, HEAD_DIM), f32)],
         compiler_params=pltpu.CompilerParams(vmem_limit_bytes=48 * 2**20),
         cost_estimate=pl.CostEstimate(flops=10**9, bytes_accessed=6 * 2**20, transcendentals=2**21),
         name="attention_forward",
     )(src, order, raw, cosine, sine)
+
+
+def heads_kernel(padded, att_out, mine, other, merged, msem, xsend, xrecv, *sems):
+    place = my_place()
+    core = place[4]
+    pl.semaphore_wait(greet(chip_neighbours(place)), 4)
+    half = SEQ // 2
+    swap = remote(
+        padded.at[pl.ds(pl.multiple_of((1 - core) * half, half), half)], other, xsend, xrecv,
+        sibling_of(place),
+    )
+    swap.start()
+    own = pltpu.make_async_copy(padded.at[pl.ds(pl.multiple_of(core * half, half), half)], mine, msem)
+    own.start()
+    own.wait()
+    swap.wait_recv()
+    merged[...] = mine[...] + other[...]
+
+    def view(p):
+        chip = p[2] * 4 + p[3]
+        return att_out.at[
+            pl.ds(pl.multiple_of(p[4] * half, half), half), pl.ds(pl.multiple_of(chip * 128, 128), 128)
+        ]
+
+    heads = RowGather(place, merged, view, half // 2, *sems)
+    heads.start()
+    heads.pass_on()
+    heads.finish()
+    swap.wait_send()
+
+
+def gather_heads(padded, number):
+    return pl.pallas_call(
+        heads_kernel,
+        out_shape=jax.ShapeDtypeStruct((SEQ, D), bf16),
+        in_specs=[ANY],
+        out_specs=ANY,
+        scratch_shapes=[pltpu.VMEM((SEQ // 2, 128), bf16)] * 3 + [DMA] * 3 + RowGather.scratch,
+        compiler_params=pltpu.CompilerParams(collective_id=number, has_side_effects=True),
+        name="gather_heads",
+    )(padded)
 
 
 def attend_back_kernel(
@@ -847,46 +929,49 @@
         ],
         axis=1,
     )
-    tokens_all, packed_all, out_all = entry(tokens, packed, w_out.reshape(16, 512), 0)
-    expert_in_all = lax.all_gather(expert_in, DP, axis=0)
-    expert_out_all = lax.all_gather(expert_out, DP, axis=0)
-    cotangent_all = lax.all_gather(cotangent, CTX, axis=0)
+    names = jnp.arange(EXPERTS, dtype=jnp.int32)
+    member = jnp.any(routes[:, :, None] == names[None, None, :], axis=1).astype(bf16)
+    member = jnp.pad(member.reshape(8, 512), ((0, 24), (0, 0)))
+    tokens_all, packed_all, out_all = entry(tokens, packed, w_out.reshape(16, 512), member, 0)
+    down_packed = expert_out.reshape(2, 8, 64, ROWS).swapaxes(1, 2).reshape(2, 64, D)
+    expert_all = lax.all_gather(jnp.concatenate([expert_in, down_packed], axis=1), DP, axis=0)
     low = packed_all[:, :, 8:, :].reshape(D, 128)
     weight = jnp.concatenate(
         [packed_all[:, :, :8, :].reshape(D, 128), low[:, :64], jnp.zeros((D, 64), bf16)], axis=1
     )
     router_weight, gain_one, gain_two = low[:, 64:96], low[:, 96], low[:, 97]
-    out_weight = out_all.reshape(HEAD_DIM, D)
+    out_weight = out_all[:, :128].reshape(N_CTX, N_DP, 8, D).swapaxes(0, 1).reshape(D, D)
+    head_weight = lax.dynamic_slice_in_dim(out_weight, ctx * HEAD_DIM, HEAD_DIM, axis=0)
+    member = out_all[:, 128:136].reshape(SEQ, EXPERTS)
 
     tokens_float = tokens.astype(f32)
     scale_one, normed_one, _ = normalize(tokens_float, gain_one)
     _, _, hidden_one = normalize(tokens_all.reshape(SEQ, D).astype(f32), gain_one)
     raw = dot(hidden_one, weight)
-    attended, query, key, value, lse = attend(src, order, raw, cosine, sine)
-    partial = dot(attended, out_weight).astype(bf16).reshape(N_CTX, ROWS, D)
-    residual = tokens_float + scatter_ctx(partial, 1)
-    scale_two, normed_two, hidden_two = normalize(residual, gain_two)
-
-    logits = dot(hidden_two, router_weight)
-    names = jnp.arange(EXPERTS, dtype=jnp.int32)
-    member = jnp.any(routes[:, :, None] == names[None, None, :], axis=1)
-    picked = jnp.where(member, logits, -1e30)
-    shifted = jnp.where(member, jnp.exp(picked - jnp.max(picked, axis=1, keepdims=True)), 0.0)
-    gates = shifted / jnp.sum(shifted, axis=1, keepdims=True)
-    high, rest = halves(gates)
-    sent = jnp.concatenate(
-        [hidden_two, high, rest, member.astype(bf16), jnp.zeros((ROWS, EXTRA - 96), bf16)], axis=1
-    )
-    all_two = gather_ctx(sent, 2)
-
-    hidden_all = all_two[:, :, :D]
-    out_part, d_part, grad_in, grad_down = experts(
-        ctx.reshape(1), all_two, cotangent_all, expert_in_all, expert_out_all
-    )
-    output = residual + scatter_ctx(out_part, 3)
-    grad_in = lax.psum_scatter(grad_in, DP, scatter_dimension=0).astype(f32)
-    grad_down = lax.psum_scatter(grad_down, DP, scatter_dimension=0).astype(f32)
-    d_sum = scatter_ctx(d_part, 4)
+    attended, padded, query, key, value, lse = attend(src, order, raw, cosine, sine)
+    attended_all = gather_heads(padded, 1)
+    residual_all = tokens_all.reshape(SEQ, D).astype(f32) + dot(attended_all, out_weight)
+    own = lambda v: lax.dynamic_slice_in_dim(v, ctx * ROWS, ROWS, axis=0)
+
+    _, _, hidden_all = normalize(residual_all, gain_two)
+    logits = dot(hidden_all, router_weight)
+    inside = member > 0.5
+    picked = jnp.where(inside, logits, -1e30)
+    shifted = jnp.where(inside, jnp.exp(picked - jnp.max(picked, axis=1, keepdims=True)), 0.0)
+    gates_all = shifted / jnp.sum(shifted, axis=1, keepdims=True)
+    high, rest = halves(gates_all)
+    facts = jnp.concatenate([high, rest, member, jnp.zeros((SEQ, EXTRA - 96), bf16)], axis=1)
+    residual = own(residual_all)
+    scale_two, normed_two, _ = normalize(residual, gain_two)
+    gates = own(gates_all)
+
+    out_sum, d_sum, grad_experts, _, _ = experts(
+        hidden_all, facts.reshape(N_CTX, ROWS, EXTRA), cotangent, expert_all, 3
+    )
+    output = residual + out_sum
+    grad_experts = lax.psum_scatter(grad_experts, DP, scatter_dimension=0).astype(f32)
+    grad_in = grad_experts[:, :ROWS]
+    grad_down = grad_experts[:, ROWS:].reshape(2, 64, 8, ROWS).swapaxes(1, 2).reshape(2, FF, ROWS)
 
     grad_top = cotangent.astype(f32)
     d_gates = d_sum[:, D : D + 32] + d_sum[:, D + 32 : D + 64]
@@ -902,7 +987,7 @@
     d_branch = all_three[:, :D]
     d_logits_all = all_three[:, D : D + 32]
 
-    d_attended = dot_last(d_branch, out_weight).astype(bf16).astype(f32)
+    d_attended = dot_last(d_branch, head_weight).astype(bf16).astype(f32)
     d_raw = attend_back(src, order, query, key, value, lse, d_attended, cosine, sine)
     d_one = dot_last(d_raw, weight).astype(bf16).reshape(N_CTX, ROWS, D)
     d_hidden_one = scatter_ctx(d_one, 6)
@@ -910,7 +995,7 @@
     input_grad = d_residual + d_norm_one
 
     grad_out_weight = dot_first(attended, d_branch)
-    own_columns = lax.dynamic_slice_in_dim(hidden_all.reshape(SEQ, D), ctx * 64, 64, axis=1)
+    own_columns = lax.dynamic_slice_in_dim(hidden_all, ctx * 64, 64, axis=1)
     grad_router = dot_first(own_columns, d_logits_all)
     second = jnp.concatenate(
         [grad_out_weight, grad_router, jnp.zeros((64, EXTRA - 32), f32)], axis=1

time: 437 us -> 388 us (0.89)
  waiting for transfers between devices: 40.3 us -> 0.04 us
  Pallas kernels: 308 us -> 278 us
  other arithmetic: 17.8 us -> 26.4 us
  matrix products: 20.1 us -> 28.5 us
    pallas_call x4 -> x1, Pallas kernels: 116 us -> 24.2 us  [scatter_ctx(): pl.pallas_call(scatter_kernel, out_shape=jax.ShapeDtypeStruct((rows, widt...]
    pallas_call x2 -> x3, Pallas kernels: 53.2 us -> 117 us  [the longest x1 81.5 us: experts(): pl.pallas_call(experts_kernel, out_shape=(jax.ShapeDtypeStruct((ROWS, D),...]
    all_gather x3 -> x1, waiting for transfers between devices: 37.7 us -> 0.01 us  [local(): lax.all_gather(jnp.concatenate([expert_in, down_packed], axis=1), DP, axi...]
    pallas_call x2 -> x1, Pallas kernels: 63.2 us -> 40.1 us  [gather_ctx(): pl.pallas_call(gather_kernel, out_shape=jax.ShapeDtypeStruct((N_CTX,) + x...]
    pallas_call x1, Pallas kernels: 38.9 us -> 58.7 us  [entry(): pl.pallas_call(entry_kernel, out_shape=(jax.ShapeDtypeStruct((N_CTX,) + x...]
    dot_general x3, matrix products: 4.23 us -> 13.3 us  [dot(): return jnp.dot(a, b, preferred_element_type=f32)]
    reshape x1 -> x4, local copies, waits for them, and re-layouts: 0.96 us -> 6.77 us  [the longest x2 5.52 us: local(): out_all[:, :128].reshape(N_CTX, N_DP, 8, D).swapaxes(0, 1).reshape(D, D)]
    unnamed x42 -> x51, local copies, waits for them, and re-layouts: 8.09 us -> 9.24 us
  transfers between devices with their start and end apart: 5 -> 2, of which waited for: 1 -> 0; matrix products, arithmetic and copies ran while one was open for 14% -> 20% of each run, Pallas kernels for 61% -> 51%
where the time goes in v3:
time: 388 us; the launch traced here: 384 us
  Pallas kernels  278 us (72%)
  local copies, waits for them, and re-layouts  36.5 us (9%)
  matrix products  28.5 us (7%)
  other arithmetic  26.4 us (7%)
  between operations  14.9 us (4%)
    pallas_call x1, Pallas kernels, experts(): pl.pallas_call(experts_kernel, out_shape=(jax.ShapeDtypeStruct((ROWS, D),...  81.5 us
    pallas_call x1, Pallas kernels, entry(): pl.pallas_call(entry_kernel, out_shape=(jax.ShapeDtypeStruct((N_CTX,) + x...  58.7 us
    pallas_call x1, Pallas kernels, gather_ctx(): pl.pallas_call(gather_kernel, out_shape=jax.ShapeDtypeStruct((N_CTX,) + x...  40.1 us
    pallas_call x1, Pallas kernels, gather_heads(): pl.pallas_call(heads_kernel, out_shape=jax.ShapeDtypeStruct((SEQ, D), bf1...  26.8 us
    pallas_call x1, Pallas kernels, scatter_ctx(): pl.pallas_call(scatter_kernel, out_shape=jax.ShapeDtypeStruct((rows, widt...  24.2 us
    pallas_call x1, Pallas kernels, grads_out(): pl.pallas_call(grads_kernel, out_shape=(jax.ShapeDtypeStruct((N_CTX, 8, w...  23.8 us
    pallas_call x1, Pallas kernels, attend_back(): pl.pallas_call(attend_back_kernel, out_shape=jax.ShapeDtypeStruct((SEQ, 2...  13.8 us
    dot_general x3, matrix products, dot(): return jnp.dot(a, b, preferred_element_type=f32)  13.3 us
  transfers between devices with their start and end apart: 2, of which 0 were waited for; matrix products, arithmetic and copies ran while one was open for 20% of the time, Pallas kernels for 51%

profile of v3, /device:TPU:1, one launch (start us, length us, event | category | flops | bytes accessed | tf_op | source)
XLA Modules:
  0.0 383.9 jit_solution(8107365593929504597)
XLA Ops:
  7.2 1.1 copy.155
  8.5 2.0 pad_maximum_fusion
  16.3 1.3 reshape.189.o_ref
  19.0 58.7 %entry_gather.1 = (bf16[16,128,1024]{2,1,0:T(8,128)(2,1)}, bf16[8,16,16,128]{3,2,1,0:T(8,128)(2,1)}, bf16[16,160,512]{2,1,0:T(8,128)(2,1)}) custom-call(bf16[128,1024]{1,0:T(8,128)(2,1)} %x_ref.1, bf16[16,16,128]{2,1,0:T(8,128)(2,1)} %maximum_maximum_fusion.5.w_ref, bf16[16,512]{1,0:T(8,128)(2,1)} %reshape.189.o_ref, bf16[32,512]{1,0:T(8,128)(2,1)} %pad_convert_fusion.m_ref), custom_call_target="tpu_custom_call" | custom-call | tf_op jit(solution)/shard_map/entry_gather/pallas_call | solution.py:355
  77.7 1.8 slice.77
  79.6 0.9 slice.79
  80.6 1.0 slice_convert_fusion.1
  82.2 3.3 fusion
  85.6 1.3 fusion.2
  87.0 2.1 copy-done.13
  89.1 2.7 fusion.25.raw_ref
  91.7 8.8 %attention_forward.1 = (bf16[2048,64]{1,0:T(8,128)(2,1)S(1)}, bf16[2048,128]{1,0:T(8,128)(2,1)S(1)}, bf16[2048,64]{1,0:T(8,128)(2,1)S(1)}, bf16[2048,64]{1,0:T(8...) custom-call(s32[32]{0:T(128)S(1)} %select_reduce_fusion.src, s32[32]{0:T(128)S(1)} %eq.31.order, ...), custom_call_target="tpu_custom_call" | custom-call | flops 1000000000 | bytes 6291456 | tf_op jit(solution)/shard_map/attention_forward/pallas_call | solution.py:758
  100.5 0.8 copy-done.2
  101.4 1.0 copy-done.5
  104.7 26.8 %gather_heads.1 = bf16[2048,1024]{1,0:T(8,128)(2,1)} custom-call(bf16[2048,128]{1,0:T(8,128)(2,1)} %copy-done.2), custom_call_target="tpu_custom_call" | custom-call | tf_op jit(solution)/shard_map/gather_heads/pallas_call | solution.py:807
  131.5 2.3 reshape.192
  133.9 3.2 copy.131
  137.3 1.0 broadcast_compare_fusion
  138.6 1.1 concatenate.52
  139.7 9.2 %multiply_reduce_fusion = (f32[2048]{0:T(1024)S(1)}, f32[2048,1024]{1,0:T(8,128)S(1)}) fusion(bf16[2048,1024]{1,0:T(8,128)(2,1)} %gather_heads.1, bf16[1024,1024]{1,0:T(8,128)(2,1)} %bitcast.91, bf16[16,128,1024]{2,1,0:T(8,128)(2,1)} %get-tuple-element.25), kind=kOutput, calls=%fused_computation.7 | convolution fusion | flops 4303353856 | bytes 18882560 | tf_op jit(solution)/shard_map/dot_general | solution.py:41
  149.0 0.9 multiply_convert_fusion
  149.9 2.3 copy-done.10
  152.2 1.4 fusion.39
  155.2 1.3 maximum_maximum_fusion.1.facts_ref
  156.5 81.5 %experts_both_ways.1 = (f32[128,1024]{1,0:T(8,128)}, f32[128,1152]{1,0:T(8,128)}, bf16[8,2,192,1024]{3,2,1,0:T(8,128)(2,1)}, bf16[16,128,1024]{2,1,0:T(8,128)(2,1)}, bf16[16,128,1152]{2,1,0:T(8,128)(2,1)}) custom-call(bf16[8,2,128,1024]{3,2,1,0:T(8,128)(2,1)} %bitcast.88, bf16[16,128,128]{2,1,0:T(8,128)(2,1)} %maximum_maximum_fusion.1.facts_ref, ...), custom_call_target="tpu_custom_call" | custom-call | flops 15000000512 | bytes 31457280 | tf_op jit(solution)/shard_map/experts_both_ways/pallas_call | solution.py:672
  238.2 1.2 multiply_reduce_fusion.3
  239.5 1.1 multiply_reduce_fusion.4
  240.6 1.0 multiply_convert_fusion.1
  241.6 1.6 multiply_reduce_fusion.1
  243.3 1.2 fusion.36
  245.4 40.1 %gather_rows.1 = bf16[16,128,1152]{2,1,0:T(8,128)(2,1)} custom-call(bf16[128,1152]{1,0:T(8,128)(2,1)} %concatenate.55.x_ref), custom_call_target="tpu_custom_call" | custom-call | tf_op jit(solution)/shard_map/gather_rows/pallas_call | solution.py:168
  285.5 3.6 fusion.7
  289.4 1.1 convert_element_type.97.do_ref
  290.5 13.8 %attention_backward.1 = bf16[2048,256]{1,0:T(8,128)(2,1)} custom-call(s32[32]{0:T(128)} %copy-done.4, s32[32]{0:T(128)} %copy-done.3, bf16[2048,64]{1,0:T(8,128)(2,1)} %copy-done.6, bf16[2048,64]{1,0:T(8,128)(2,1)} %copy-done.7, bf16[2048,64]{1,0:T(8,128)(2,1)} %copy-done.8, f32[2048,1]{1,0:T(8,128)} %copy-done.5, f32[2048,64]{1,0:T(8,128)} %convert_element_type.97.do_ref, ...), custom_call_target="tpu_custom_call" | custom-call | flops 3000000000 | bytes 6291456 | tf_op jit(solution)/shard_map/attention_backward/pallas_call | solution.py:853
  304.2 2.6 fusion.40
  306.8 1.0 copy.137
  307.8 2.5 convolution_convert_fusion
  310.4 24.2 %scatter_rows.1 = f32[128,1024]{1,0:T(8,128)S(1)} custom-call(bf16[8,2,128,1024]{3,2,1,0:T(8,128)(2,1)S(1)} %bitcast.78), custom_call_target="tpu_custom_call" | custom-call | tf_op jit(solution)/shard_map/scatter_rows/pallas_call | solution.py:285
  334.9 0.9 copy.138
  335.7 0.9 copy.139
  336.6 1.7 fusion.22
  338.4 3.1 fusion.3
  341.6 1.3 maximum_maximum_fusion.2.a_ref
  342.9 23.8 %sum_grads.1 = (f32[16,8,256]{2,1,0:T(8,128)S(1)}, f32[8,8,1152]{2,1,0:T(8,128)S(1)}) custom-call(bf16[8,128,256]{2,1,0:T(8,128)(2,1)S(1)} %maximum_maximum_fusion.2.a_ref, f32[8,8,1152]{2,1,0:T(8,128)S(1)} %bitcast.79), custom_call_target="tpu_custom_call" | custom-call | tf_op jit(solution)/shard_map/sum_grads/pallas_call | solution.py:463
  370.9 2.4 fusion.19
  373.3 1.3 bitcast_convert_fusion
  374.7 1.1 slice.108
  375.9 0.9 copy.144
  (118 shorter events, 18.9 us)
Async XLA Ops:
  7.2 149.3 %all-gather.3.cloned.1.call-start = ((), (), s32[]{:S(2)}) async-start(), calls=%async_computation.2 | async-start | bytes 7077888 | tf_op jit(solution)/shard_map/all_gather | solution.py:937
  10.5 362.8 %reduce-scatter.2.cloned.1.call-start = ((), (), s32[]{:S(2)}) async-start(), calls=%async_computation.1 | async-start | bytes 7077888 | tf_op jit(solution)/shard_map/reduce_scatter | solution.py:972
  15.4 66.5 %copy-start.23 = (s32[16]{0:T(128)S(1)}, s32[16]{0:T(128)}, u32[]{:S(2)}) copy-start(s32[16]{0:T(128)} %param.17) | copy-start | bytes 196
  77.7 2.8 copy-start.22
  80.6 6.3 %copy-start.20 = (bf16[8,16,8,128]{3,2,1,0:T(8,128)(2,1)}, bf16[8,16,8,128]{3,2,1,0:T(8,128)(2,1)S(1)}, u32[]{:S(2)}) copy-start(bf16[8,16,8,128]{3,2,1,0:T(8,128)(2,1)S(1)} %get-tuple-element.49) | copy-start | bytes 786436
  82.1 9.6 %copy-start.3 = (s32[32]{0:T(128)}, s32[32]{0:T(128)S(1)}, u32[]{:S(2)}) copy-start(s32[32]{0:T(128)S(1)} %eq.31.order) | copy-start | bytes 388
  82.1 3.5 copy-start.9
  82.2 9.5 %copy-start.4 = (s32[32]{0:T(128)}, s32[32]{0:T(128)S(1)}, u32[]{:S(2)}) copy-start(s32[32]{0:T(128)S(1)} %select_reduce_fusion.src) | copy-start | bytes 388
  86.9 2.1 copy-start.13
  86.9 4.8 %copy-start = (f32[2048,128]{1,0:T(8,128)S(1)}, f32[2048,128]{1,0:T(8,128)}, u32[]{:S(2)}) copy-start(f32[2048,128]{1,0:T(8,128)} %constant.63.clone.cos_ref) | copy-start | bytes 3145732
  86.9 4.8 %copy-start.1 = (f32[2048,128]{1,0:T(8,128)S(1)}, f32[2048,128]{1,0:T(8,128)}, u32[]{:S(2)}) copy-start(f32[2048,128]{1,0:T(8,128)} %constant.64.clone.sin_ref) | copy-start | bytes 3145732
  100.5 0.9 copy-start.2
  101.4 1.0 copy-start.5
  102.3 0.8 copy-start.6
  103.1 0.8 copy-start.7
  103.9 0.8 copy-start.8
  133.9 3.2 copy-start.16
  149.0 3.2 copy-start.10
  152.2 2.1 copy-start.11
  153.6 1.6 copy-start.15
  238.0 1.3 copy-start.12
  238.0 5.3 %copy-start.18 = (bf16[128,1024]{1,0:T(8,128)(2,1)S(1)}, bf16[128,1024]{1,0:T(8,128)(2,1)}, u32[]{:S(2)}) copy-start(bf16[128,1024]{1,0:T(8,128)(2,1)} %cot_ref.1) | copy-start | bytes 786436
  290.5 13.8 %copy-start.14 = (bf16[2048,1024]{1,0:T(8,128)(2,1)S(1)}, bf16[2048,1024]{1,0:T(8,128)(2,1)}, u32[]{:S(2)}) copy-start(bf16[2048,1024]{1,0:T(8,128)(2,1)} %copy-done.13) | copy-start | bytes 12582916
  304.2 3.6 copy-start.21
  334.6 7.0 %copy-start.17 = (bf16[1024,192]{1,0:T(8,128)(2,1)S(1)}, bf16[1024,192]{1,0:T(8,128)(2,1)}, u32[]{:S(2)}) copy-start(bf16[1024,192]{1,0:T(8,128)(2,1)} %copy.137) | copy-start | bytes 1179652
  338.4 32.5 %copy-start.19 = (bf16[128,1024]{1,0:T(8,128)(2,1)S(1)}, bf16[128,1024]{1,0:T(8,128)(2,1)}, u32[]{:S(2)}) copy-start(bf16[128,1024]{1,0:T(8,128)(2,1)} %cot_ref.1) | copy-start | bytes 786436
Sparse Core Ops, SparseCore 0:
  10.6 92.9 all-gather.2
  238.2 85.0 reduce-scatter.1
